TPU v7x, 32 devices: a whole 2x2x4 slice. The times are simulated.
32 devices in a mesh: dp: 8 (over z, x), tensor: 4 (over y, core).
Axes of the slice: x: 2, y: 2, z: 4, core: 2. Of those that a mesh axis runs over, the one named last changes fastest.
Arguments:
- tokens: bfloat16 [32, 1152, 256], P('dp'), may hold values from -6 to 6
- lengths: int32 [32], P('dp'), may hold values from 288 to 1152, as said below
- row_mask: int32 [32, 12], P('dp'), may hold values 0 or 1
- cotangent: bfloat16 [32, 1152, 256], P('dp'), may hold values from -6 to 6
- w_qkv: bfloat16 [256, 768], P(('dp', 'tensor')), may hold values from -0.375 to 0.375
- w_out: bfloat16 [256, 256], P(('dp', 'tensor')), may hold values from -1.5 to 1.5
- gains: bfloat16 [2, 256], P(None, ('dp', 'tensor')), may hold values from 0.5 to 1.5
- biases: bfloat16 [3, 256], P(None, ('dp', 'tensor')), may hold values from -2 to 2
- w_up: bfloat16 [256, 1024], P('dp', 'tensor'), may hold values from -0.375 to 0.375
- w_down: bfloat16 [1024, 256], P('tensor', 'dp'), may hold values from -0.1875 to 0.1875
Outputs:
- layer_out: bfloat16 [32, 1152, 256], P('dp')
- grad_tokens: float32 [32, 1152, 256], P('dp')
- grad_qkv: float32 [256, 768], P(('dp', 'tensor'))
- grad_wout: float32 [256, 256], P(('dp', 'tensor'))
- grad_gains: float32 [2, 256], P(None, ('dp', 'tensor'))
- grad_biases: float32 [3, 256], P(None, ('dp', 'tensor'))
- grad_up: float32 [256, 1024], P('dp', 'tensor')
- grad_down: float32 [1024, 256], P('tensor', 'dp')
Inputs may be any that keep to these rules, and one draw needn't show every extreme that they name: `lengths`: some image has all 1152 tokens real.
All inputs are finite; a program needn't handle non-finite values. No bound on the sum of `row_mask` on one device may be relied on, other than what follows from the above.
Results may differ from a plain program's by a relative error of at most 0.013.
Values may be sent and summed in bfloat16 or wider, within the bound.
No kernel may reach another device: no remote copies, remote signals or barrier semaphores. Data moves between devices by JAX's collectives and lax.ppermute only.
A program may use at most 128 MiB of HBM per device.

v0:
```python
import functools

import jax
import jax.numpy as jnp
from jax import lax
from jax.experimental import pallas as pl
from jax.experimental.pallas import tpu as pltpu
from jax.sharding import PartitionSpec as P

HEADS = 2
WIN = 96
F32 = jnp.float32
BF16 = jnp.bfloat16
VDP, VT = 8, 4
CHIPS = VDP * VT // 2
MIB = 1 << 20

NN = ((1,), (0,))
NT = ((1,), (1,))
TN = ((0,), (0,))


def dot(a, b, dims):
    return lax.dot_general(a, b, (dims, ((), ())), preferred_element_type=F32)


def twist(i):
    return (i & 1) * 4 + (i >> 1)


def turn(i):
    return ((i & 1) << 2) | (i & 2) | ((i & 4) >> 2)


def spot(m):
    return (m % 2) * VDP + twist(m // 2)


def norm_parts(values):
    center = values - jnp.mean(values, -1, keepdims=True)
    inv = lax.rsqrt(jnp.mean(center * center, -1, keepdims=True) + 1e-05)
    return center * inv, inv


def norm_back(grad, xhat, inv, gain):
    scaled = grad * gain
    return inv * (
        scaled
        - jnp.mean(scaled, -1, keepdims=True)
        - xhat * jnp.mean(scaled * xhat, -1, keepdims=True)
    )


def gelu_both(u):
    c = 0.7978845608028654
    u2 = u * u
    t = jnp.tanh(u * (c + (c * 0.044715) * u2))
    half = 0.5 + 0.5 * t
    value = u * half
    slope = half + (value - value * half) * (2 * c + (6 * c * 0.044715) * u2)
    return value, slope


def apart(both, hs):
    blocks = []
    for h in range(HEADS):
        parts = [jnp.zeros((WIN, hs), BF16)] * HEADS
        parts[h] = both[:, h * hs : (h + 1) * hs]
        blocks.append(jnp.concatenate(parts, 1))
        blocks.append(jnp.zeros((hs - WIN, HEADS * hs), BF16))
    return jnp.concatenate(blocks, 0)


def pack_kernel(me, *refs):
    sources, packed, held, sems = refs[:6], refs[6], refs[7:13], refs[13]
    copies = [pltpu.make_async_copy(a, b, sems.at[n]) for n, (a, b) in enumerate(zip(sources, held))]
    for copy in copies:
        copy.start()
    qkv, out, gains, biases, up, down = held
    small, width = out.shape
    tall = up.shape[0]
    lane = lax.broadcasted_iota(jnp.int32, (1, width), 1)
    mine = lane // small == me[0]
    for copy in copies:
        copy.wait()
    for part in range(3):
        packed[0, part * small : (part + 1) * small] = qkv[:, part * width : (part + 1) * width]
    packed[0, 3 * small : 4 * small] = out[...]
    rows = [gains[0:1], gains[1:2], biases[0:1], biases[1:2], biases[2:3]]
    vals = jnp.concatenate(rows + [jnp.zeros((3, small), BF16)], 0).astype(F32)
    wide = jnp.concatenate([vals] * (width // small), 1)
    at = 4 * small + 8
    packed[0, 4 * small : at] = jnp.where(mine, wide, 0.0).astype(BF16)
    packed[0, at : at + tall] = up[...]
    packed[0, at + tall :] = down[...]


def turn_kernel(me, cot, tokens, cot_ref, cot_t, x_ref, sems):
    own = cot_ref.shape[0]
    at = pl.ds(lax.rem(me[0], 2) * own, own)
    copies = [
        pltpu.make_async_copy(cot.at[at], cot_ref, sems.at[0]),
        pltpu.make_async_copy(tokens.at[at], x_ref, sems.at[1]),
    ]
    for copy in copies:
        copy.start()
    size = 256 if own % 256 == 0 else own
    copies[0].wait()
    for n in range(own // size):
        part = slice(n * size, (n + 1) * size)
        cot_t[:, part] = cot_ref[part].T
    copies[1].wait()


def first_norm_kernel(x_ref, xhat_ref, inv_ref, xhat_t):
    own, width = x_ref.shape
    ones = jnp.full((width, width), 1.0 / width, BF16)
    size = 256 if own % 256 == 0 else own
    for n in range(own // size):
        part = slice(n * size, (n + 1) * size)
        x = x_ref[part]
        center = x.astype(F32) - dot(x, ones, NN)
        inv = lax.rsqrt(dot((center * center).astype(BF16), ones, NN) + 1e-05)
        xhat = center * inv
        xhat_ref[part] = xhat
        inv_ref[part] = inv[:, :1]
        xhat_t[:width, part] = xhat.astype(BF16).T
        xhat_t[width:, part] = jnp.ones((16, size), BF16)


def attend_kernel(
    per, me, virt, lens, live, x_ref, xhat_ref, held, got,
    qkv_ref, prob_ref, o_ref, x1_ref, wqkv, wout, vec,
):
    tokens, width = x_ref.shape
    rows = tokens // WIN
    hs = width // HEADS
    here = twist(virt[0] // 4)
    y_own = (virt[0] // 2) % 2
    first = virt[0] % 2 == 0
    for m in range(CHIPS):
        k = spot(m) ^ (here + y_own * VDP)
        at = pl.ds(pl.multiple_of(k * 32, 32), 32)
        a = held[at].astype(F32)
        b = got[at].astype(F32)
        even = jnp.where(first, a, b)
        odd = jnp.where(first, b, a)
        for part in range(3):
            both = jnp.concatenate([even[part * 8 : part * 8 + 8], odd[part * 8 : part * 8 + 8]], 0)
            wqkv[m * 16 : m * 16 + 16, part * width : (part + 1) * width] = both.astype(BF16)
        both = jnp.concatenate([even[24:32], odd[24:32]], 0)
        wout[m * 16 : m * 16 + 16] = both.astype(BF16)
    total = held[CHIPS * 32 :].astype(F32) + got[CHIPS * 32 :].astype(F32)
    vec[...] = total
    scale = hs**-0.5
    ii = lax.broadcasted_iota(jnp.int32, (WIN, hs), 0)
    jj = lax.broadcasted_iota(jnp.int32, (WIN, hs), 1)
    same = ii == jj
    image_rows = live.shape[1]
    base = lax.rem(me[0], 2) * rows

    def enter(c):
        part = slice(c * per * WIN, (c + 1) * per * WIN)
        h1 = (xhat_ref[part] * total[0:1] + total[2:3]).astype(BF16)
        qkv = dot(h1, wqkv[...], NN).astype(BF16)
        qkv_ref[part] = qkv
        scores = []
        for r in range(per):
            at = slice(r * WIN, (r + 1) * WIN)
            scores.append(dot(qkv[at, :width], apart(qkv[at, width : 2 * width], hs), NT))
        return qkv, scores

    ahead = enter(0)
    for c in range(rows // per):
        qkv, scores = ahead
        if c + 1 < rows // per:
            ahead = enter(c + 1)
        part = slice(c * per * WIN, (c + 1) * per * WIN)
        probs = []
        for r in range(per):
            row = base + c * per + r
            image = row // image_rows
            inside = row - image * image_rows
            reach = jnp.where(live[image, inside] == 1, lens[image] - inside * WIN, 0)
            allowed = same | (jj < jnp.minimum(ii, reach))
            heads = []
            for h in range(HEADS):
                s = jnp.where(allowed, scores[r][:, h * hs : (h + 1) * hs], -1e30)
                e = jnp.exp((s - jnp.max(s, -1, keepdims=True)) * scale)
                heads.append((e * (1.0 / jnp.sum(e, -1, keepdims=True))).astype(BF16))
            probs.append(jnp.concatenate(heads, 1))
        mixed = []
        for r in range(per):
            at = slice(r * WIN, (r + 1) * WIN)
            mixed.append(dot(probs[r], apart(qkv[at, 2 * width :], hs), NN).astype(BF16))
        o = jnp.concatenate(mixed, 0)
        for n, p in enumerate(probs):
            prob_ref[c * per + n] = p
        o_ref[part] = o
        x1_ref[part] = x_ref[part].astype(F32) + dot(o, wout[...], NN)


def join(virt, blocks, n, up, down_t):
    tall = blocks.shape[1] // 2
    width = up.shape[0]
    here = twist(virt[0] // 4)
    for i in range(VDP):
        k = twist(i) ^ here
        at = slice(i * tall, (i + 1) * tall)
        cols = slice(n * width, (n + 1) * width)
        up[at, cols] = blocks[k, :tall]
        down_t[at, cols] = blocks[k, tall:]


def hidden_units(h2, dyb, up, down_t):
    u = dot(h2, up[...], NN).astype(BF16)
    da = dot(dyb, down_t[...], NN).astype(BF16)
    a, slope = gelu_both(u)
    return a, da * slope


def hidden_near_kernel(
    per, virt, x1_ref, cot_ref, cot_t, vec, own, got,
    h2_ref, xhat_ref, inv_ref, f_ref, dh2_ref, keep, send,
    a_ref, du_ref, h2_t, up, down_t, up_t, down,
):
    tokens, width = x1_ref.shape
    size = per * WIN
    join(virt, own, 0, up, down_t)
    join(virt, got, 1, up, down_t)
    up_t[...] = up[...].T
    down[...] = down_t[...].T
    for c in range(tokens // size):
        part = slice(c * size, (c + 1) * size)
        x1 = x1_ref[part]
        xhat, inv = norm_parts(x1)
        xhat_ref[part] = xhat
        inv_ref[part] = inv
        h2 = (xhat * vec[1:2] + vec[3:4]).astype(BF16)
        h2_ref[part] = h2
        h2_t[:, part] = h2.T
        a, du = hidden_units(h2, cot_ref[part], up, down_t)
        a_ref[part] = a
        du_ref[part] = du
        f_ref[part] = x1 + vec[4:5] + dot(a, down[...], NN)
        dh2_ref[part] = dot(du, up_t[...], NN)
    gdown = dot(cot_t[...], a_ref[...], NN)
    gup = dot(h2_t[...], du_ref[...], NN)
    tall = width // VDP
    here = turn(virt[0] // 4)
    for i in range(VDP):
        at = slice(i * tall, (i + 1) * tall)
        k = turn(i) ^ here
        keep[k, :tall] = gup[at, :width]
        keep[k, tall:] = gdown[at, :width]
        send[k, :tall] = gup[at, width:].astype(BF16)
        send[k, tall:] = gdown[at, width:].astype(BF16)


def hidden_far_kernel(
    per, virt, cot_ref, vec, own, got, h2_ref, xhat_ref, inv_ref, f_ref, dh2_ref, o_ref,
    y_ref, dx1_ref, g_ref, gout, gvec,
    o_t, up, down_t, up_t, down,
):
    tokens, width = h2_ref.shape
    size = per * WIN
    join(virt, own, 0, up, down_t)
    join(virt, got, 1, up, down_t)
    up_t[...] = up[...].T
    down[...] = down_t[...].T
    sums = [jnp.zeros((1, width), F32)] * 3
    for c in range(tokens // size):
        part = slice(c * size, (c + 1) * size)
        o_t[:, part] = o_ref[part].T
        a, du = hidden_units(h2_ref[part], cot_ref[part], up, down_t)
        y_ref[part] = (f_ref[part] + dot(a, down[...], NN)).astype(BF16)
        dh2 = dh2_ref[part] + dot(du, up_t[...], NN)
        dy = cot_ref[part].astype(F32)
        xhat = xhat_ref[part]
        dx1 = dy + norm_back(dh2, xhat, inv_ref[part], vec[1:2])
        dx1_ref[part] = dx1
        g_ref[part] = dx1.astype(BF16)
        for n, term in enumerate((dh2 * xhat, dh2, dy)):
            sums[n] = sums[n] + jnp.sum(term, 0, keepdims=True)
    gout[...] = dot(o_t[...], g_ref[...], NN)
    zero = jnp.zeros((1, width), F32)
    gvec[...] = jnp.concatenate([zero, sums[0], zero, sums[1], sums[2], zero, zero, zero], 0)


def own_rows(virt, i, other):
    core = virt[0] % 2
    core = 1 - core if other else core
    return pl.ds(pl.multiple_of(i * 32 + ((virt[0] // 2) % 2) * 16 + core * 8, 8), 8)


def back_kernel(
    per, virt, qkv_ref, prob_ref, g_ref, xhat_t, wqkv, wout, vec, gout, gvec,
    dqkv, keep, send, vec_sums,
    gqkv,
):
    tokens, width = g_ref.shape
    hs = width // HEADS
    scale = hs**-0.5
    every = [(r, h) for r in range(tokens // WIN) for h in range(HEADS)]
    groups = [every[n : n + 2 * per] for n in range(0, len(every), 2 * per)]

    def piece(ref, r, h, part=0):
        return ref[r * WIN : (r + 1) * WIN, part * width + h * hs : part * width + (h + 1) * hs]

    def enter(pairs):
        r = pairs[0][0]
        do = dot(g_ref[r * WIN : (r + per) * WIN], wout[...], NT).astype(BF16)
        dos = [do[(n - r) * WIN : (n - r + 1) * WIN, h * hs : (h + 1) * hs] for n, h in pairs]
        probs = [prob_ref[r, :, h * hs : h * hs + WIN] for r, h in pairs]
        dps = [dot(a, piece(qkv_ref, r, h, 2), NT) for a, (r, h) in zip(dos, pairs)]
        dvs = [dot(p, a, TN).astype(BF16) for p, a in zip(probs, dos)]
        return probs, dps, dvs

    ahead = enter(groups[0])
    for place, pairs in enumerate(groups):
        probs, dps, dvs = ahead
        if place + 1 < len(groups):
            ahead = enter(groups[place + 1])
        dss = []
        for p, dp in zip(probs, dps):
            pf = p.astype(F32)
            ds = pf * (dp - jnp.sum(dp * pf, -1, keepdims=True)) * scale
            dss.append(ds.astype(BF16))
        dqs = [dot(ds, piece(qkv_ref, r, h, 1), NN).astype(BF16) for ds, (r, h) in zip(dss, pairs)]
        dks = [dot(ds, piece(qkv_ref, r, h, 0), TN).astype(BF16) for ds, (r, h) in zip(dss, pairs)]
        for n, (r, h) in enumerate(pairs):
            for part, values in enumerate((dqs, dks, dvs)):
                at = slice(part * width + h * hs, part * width + (h + 1) * hs)
                dqkv[r * WIN : (r + 1) * WIN, at] = values[n]
    both = dot(xhat_t[...], dqkv[...], NN)
    grad, total = both[:width], both[width : width + 1]
    w = wqkv[...].astype(F32)
    cols = jnp.concatenate([
        jnp.broadcast_to(jnp.sum(w * grad, -1, keepdims=True), (width, 64)),
        jnp.broadcast_to(jnp.sum(w * total, -1, keepdims=True), (width, 64)),
    ], 1)
    lines = cols.T
    gain, from_total = lines[0:1], lines[64:65]
    vec_t = vec[...].T
    gqkv[...] = grad * vec_t[:, 0:1] + total * vec_t[:, 2:3]
    rest = gvec[...]
    sums = jnp.concatenate([gain, rest[1:2], from_total, rest[3:]], 0)
    here = twist(virt[0] // 4)
    for i in range(VDP):
        k = twist(i) ^ here
        mine, other = own_rows(virt, i, 0), own_rows(virt, i, 1)
        theirs = []
        for part in range(3):
            at = slice(part * width, (part + 1) * width)
            keep[k, part * 8 : part * 8 + 8] = gqkv[mine, at]
            theirs.append(gqkv[other, at])
        keep[k, 24:] = gout[mine]
        at = pl.ds(pl.multiple_of(k * 32, 32), 32)
        send[at] = jnp.concatenate(theirs + [gout[other]], 0).astype(BF16)
    vec_sums[...] = sums
    send[VDP * 32 :] = sums.astype(BF16)


def token_grad_kernel(per, me, dqkv, wqkv, vec, xhat_ref, inv_ref, dx1_ref, y, y_near, gx, gxb, out, turned, sems):
    own = dqkv.shape[0]
    size = per * WIN
    copies = []
    for n, source in enumerate((y, y_near)):
        at = pl.ds((lax.rem(me[0], 2) ^ n) * own, own)
        copies.append(pltpu.make_async_copy(source, out.at[at], sems.at[n]))
        copies[-1].start()
    turned[...] = wqkv[...].T
    for c in range(own // size):
        part = slice(c * size, (c + 1) * size)
        dh1 = dot(dqkv[part], turned[...], NN)
        values = dx1_ref[part] + norm_back(dh1, xhat_ref[part], inv_ref[part], vec[0:1])
        gx[part] = values
        gxb[part] = values.astype(BF16)
    for copy in copies:
        copy.wait()


def place_kernel(per, me, mine, theirs, out, wide, sems):
    own = theirs.shape[0]
    size = per * WIN
    here = lax.rem(me[0], 2) * own
    copies = [pltpu.make_async_copy(mine, out.at[pl.ds(here, own)], sems.at[own // size])]
    copies[0].start()
    for c in range(own // size):
        part = pl.ds(c * size, size)
        wide[part] = theirs[part].astype(F32)
        at = pl.ds(own - here + c * size, size)
        copies.append(pltpu.make_async_copy(wide.at[part], out.at[at], sems.at[c]))
        copies[-1].start()
    for copy in copies:
        copy.wait()


def finish_kernel(me, keep_a, keep_b, sums, *refs):
    qkv, out, gains, biases, up, down = refs[3:]
    small, width = out.shape
    tall = up.shape[0]
    high = 4 * small + 8
    total, vec = keep_a[0], sums[...]
    for got in refs[:3]:
        total = total + got[: 4 * small].astype(F32)
        vec = vec + got[4 * small : high].astype(F32)
    units = keep_b[0] + refs[1][high:].astype(F32)
    for part in range(3):
        qkv[:, part * width : (part + 1) * width] = total[part * small : (part + 1) * small]
    out[...] = total[3 * small :]
    vec = pltpu.roll(vec, width - me[0] * small, 1)[:, :small]
    gains[...] = vec[:2]
    biases[...] = vec[2:5]
    up[...] = units[:tall]
    down[...] = units[tall:]


def swap(block, axis, bit):
    size = lax.axis_size(axis)
    return lax.ppermute(block, axis, [(i, i ^ bit) for i in range(size)])


def steps_of(axis):
    return [(axis, 1 << k) for k in reversed(range(lax.axis_size(axis).bit_length() - 1))]


def after(value, other):
    return lax.optimization_barrier((value, other))[0]


def merge(pieces):
    vec = sum(piece[-8:] for piece in pieces)
    return jnp.concatenate([piece[:-8] for piece in pieces] + [vec], 0)


def halves(held):
    half = held.shape[0] // 2
    return held[:half], held[half:].astype(BF16)


def fold_step(keep, send, axis, bit, past=None):
    got = swap(send, axis, bit)
    return keep + (got if past is None else after(got, past)).astype(F32)


def bit_reverse(index, count):
    out = 0 * index
    for k in range(count):
        out = out | (((index >> k) & 1) << (count - 1 - k))
    return out


def by_device(block, me):
    blocks = block[None]
    for axis, bit in steps_of("dp") + steps_of("tensor"):
        blocks = jnp.concatenate([blocks, swap(blocks, axis, bit)], 0)
    count = blocks.shape[0]
    order = jnp.arange(count, dtype=jnp.int32) ^ me
    return jnp.take(blocks, bit_reverse(order, count.bit_length() - 1), axis=0)


def other_pack(w_qkv, w_out, gains, biases, w_up, w_down, me):
    small, width = w_out.shape
    qkv = w_qkv.reshape(small, 3, width).transpose(1, 0, 2).reshape(3 * small, width)
    rows = jnp.concatenate([gains, biases], 0)
    place = jnp.zeros((8, width), BF16)
    place = lax.dynamic_update_slice(place, rows, (jnp.int32(0), me * small))
    return jnp.concatenate([qkv, w_out, place], 0), jnp.concatenate([w_up, w_down.T], 0)


def other_blocks(a, b, me, n_dp, n_t):
    a = by_device(a, me)
    b = by_device(b, me)
    width = a.shape[2]
    count = n_dp * n_t
    small = width // count
    big = width // (VDP * VT)
    mats = a[:, : 4 * small].reshape(count, 4, small, width).transpose(1, 0, 2, 3)
    mats = mats.reshape(4, VDP * VT, big, width).transpose(1, 0, 2, 3).reshape(VDP * VT, 4 * big, width)
    vec = jnp.sum(a[:, 4 * small :].astype(F32), 0).astype(BF16)
    a = mats
    tall = width // n_dp
    b = b.reshape(n_dp, VT, 2, tall, width).transpose(1, 2, 0, 3, 4)
    b = b.reshape(VT, 2, VDP, width // VDP, width).transpose(2, 0, 1, 3, 4)
    b = b.reshape(VDP * VT, 2 * (width // VDP), width)

    y_own = (me // 2) % 2

    def placed(blocks):
        pairs = blocks.reshape((CHIPS, 2) + blocks.shape[1:])
        chips = sorted(range(CHIPS), key=spot)
        pairs = jnp.stack([pairs[m] for m in chips], 0)
        pairs = jnp.where(y_own == 1, jnp.roll(pairs, VDP, 0), pairs)
        return pairs[:, 0], pairs[:, 1]

    held_a, got_a = (part.reshape(-1, width) for part in placed(a))
    held_a = jnp.concatenate([held_a, vec], 0)
    got_a = jnp.concatenate([got_a, jnp.zeros_like(vec)], 0)
    return (held_a, got_a) + placed(b)


def other_reduce(pair_a, pair_b, sums, me, n_dp, n_t):
    count = n_dp * n_t
    y_own = (me // 2) % 2

    def whole(keep, send, order):
        pairs = jnp.stack([keep, send.astype(F32)], 1)
        pairs = jnp.stack([pairs[order(i)] for i in range(VDP)], 0)
        none = jnp.zeros_like(pairs)
        both = jnp.stack([jnp.where(y_own == y, pairs, none) for y in range(2)], 1)
        return both.reshape((VDP * VT,) + keep.shape[1:])

    def rows_of(blocks, parts):
        big = blocks.shape[1] // parts
        mats = blocks.reshape(VDP * VT, parts, big, -1).transpose(1, 0, 2, 3)
        mats = mats.reshape(parts, count, VDP * VT * big // count, -1).transpose(1, 0, 2, 3)
        return mats.reshape(count, -1, blocks.shape[2])

    a, b = whole(*pair_a, twist), whole(*pair_b, turn)
    width = a.shape[2]
    tall, high = width // n_dp, width // VDP
    cols = b.reshape(VDP, VT, 2, high, width).transpose(1, 2, 0, 3, 4)
    cols = cols.reshape(VT, 2, n_dp, tall, width).transpose(2, 0, 1, 3, 4)
    cols = cols.reshape(count, 2 * tall, width)
    vec = jnp.broadcast_to(jnp.where(y_own == 0, sums, 0.0)[None], (count,) + sums.shape)
    a = jnp.concatenate([rows_of(a, 4), vec], 1)
    results = []
    for blocks in (a, cols):
        blocks = jnp.take(blocks, jnp.arange(count, dtype=jnp.int32) ^ me, axis=0)
        for axis, bit in reversed(steps_of("dp") + steps_of("tensor")):
            pairs = blocks.reshape((-1, 2) + blocks.shape[1:])
            got = swap(pairs[:, 1].astype(BF16), axis, bit)
            blocks = pairs[:, 0] + got.astype(F32)
        results.append(blocks[0])
    return results


def struct(shape, dtype):
    return jax.ShapeDtypeStruct(shape, dtype)


def call(kernel, name, args, outs, scratch=(), flops=0, limit=8, hbm_outs=True):
    args = [a if isinstance(a, tuple) else (a, pltpu.VMEM) for a in args]
    moved = sum(a.size * a.dtype.itemsize for a, _ in args)
    spaces = [pl.ANY if hbm_outs and isinstance(o, jax.ShapeDtypeStruct) else pltpu.VMEM for o in outs]
    return pl.pallas_call(
        kernel,
        name=name,
        out_shape=outs,
        in_specs=[pl.BlockSpec(memory_space=space) for _, space in args],
        out_specs=[pl.BlockSpec(memory_space=space) for space in spaces],
        scratch_shapes=list(scratch),
        compiler_params=pltpu.CompilerParams(vmem_limit_bytes=limit * MIB),
        cost_estimate=pl.CostEstimate(flops=flops, bytes_accessed=moved, transcendentals=0),
    )(*[a for a, _ in args])


def on_device(tokens, lengths, row_mask, cotangent, w_qkv, w_out, gains, biases, w_up, w_down):
    images, seq_len, width = tokens.shape
    n_dp, n_t = lax.axis_size("dp"), lax.axis_size("tensor")
    index = lax.axis_index("dp") * n_t + lax.axis_index("tensor")
    me = index.astype(jnp.int32).reshape(1)
    usual = (n_dp, n_t) == (VDP, VT)
    virt = me if usual else (index // 2 % 2 * 2).astype(jnp.int32).reshape(1)
    small = width // (n_dp * n_t)
    tall = width // n_dp
    own = images * seq_len // 2
    rows = own // WIN
    per = 12 if rows % 12 == 0 else 1
    some = 6 if rows % 6 == 0 else 1
    less = 4 if rows % 4 == 0 else 1
    smem = pltpu.SMEM
    weights = (w_qkv, w_out, gains, biases, w_up, w_down)
    token_mm = 2 * own * width
    hbm = pltpu.HBM

    def in_hbm(array):
        return (pltpu.with_memory_space_constraint(array, hbm), hbm)

    def first_norm(x):
        return call(
            first_norm_kernel,
            "first_norm",
            [x],
            [
                pltpu.VMEM((own, width), F32),
                pltpu.VMEM((own, 1), F32),
                pltpu.VMEM((width + 16, own), BF16),
            ],
            limit=4,
        )

    def fetch(me):
        flat = [array.reshape(images * seq_len, width) for array in (cotangent, tokens)]
        return call(
            turn_kernel,
            "turn",
            [(me, smem)] + [in_hbm(array) for array in flat],
            [
                pltpu.VMEM((own, width), BF16),
                pltpu.VMEM((width, own), BF16),
                pltpu.VMEM((own, width), BF16),
            ],
            [pltpu.SemaphoreType.DMA((2,))],
            limit=4,
        )

    if usual:
        weights = (w_qkv, w_out, gains, biases, w_up, w_down.T)
        high = 4 * small + 8
        packed = call(
            pack_kernel,
            "pack",
            [(me, smem)] + [in_hbm(w) for w in weights],
            [pltpu.VMEM((1, high + 2 * tall, width), BF16)],
            [pltpu.VMEM(w.shape, BF16) for w in weights] + [pltpu.SemaphoreType.DMA((6,))],
        )[0]
        planes = [packed] + [swap(packed, "dp", bit) for bit in (2, 4, 6)]
        cot, cot_t, x = fetch(after(me, packed))
        planes[3] = after(planes[3], cot)
        held_a = merge([plane[0, :high] for plane in planes])
        b = jnp.concatenate([plane[:, high:] for plane in planes], 0)
        far_b = swap(b, "tensor", 2)
        held_a = merge([held_a, swap(held_a, "dp", 1)])
        b = jnp.concatenate([b, swap(b, "dp", 1)], 0)
        xhat1, inv1, xhat_t = first_norm(after(x, (held_a, far_b)))
        held_a = merge([held_a, after(swap(held_a, "tensor", 2), (b, xhat1))])
        far_x = swap(far_b, "dp", 1)
        got_a = swap(held_a, "tensor", 1)
        got_b = swap(b, "tensor", 1)
    else:
        held_a, got_a, held_b, got_b = other_blocks(*other_pack(*weights, index), index, n_dp, n_t)
        b, far_b = held_b[:VDP], held_b[VDP:]
        got_b, got_far = got_b[:VDP], got_b[VDP:]
        cot, cot_t, x = fetch(me)
        xhat1, inv1, xhat_t = first_norm(x)
    qkv, prob, o, x1, wqkv, wout, vec = call(
        functools.partial(attend_kernel, some),
        "attend",
        [(me, smem), (virt, smem), (lengths, smem), (row_mask, smem), x, xhat1, held_a, got_a],
        [
            pltpu.VMEM((own, 3 * width), BF16),
            pltpu.VMEM((rows, WIN, width), BF16),
            pltpu.VMEM((own, width), BF16),
            pltpu.VMEM((own, width), F32),
            pltpu.VMEM((width, 3 * width), BF16),
            pltpu.VMEM((width, width), BF16),
            pltpu.VMEM((8, width), F32),
        ],
        flops=token_mm * (4 * width + 2 * WIN),
    )
    tall_b = 2 * (width // VDP)
    mats = [pltpu.VMEM((width, 2 * width), BF16)] * 2 + [pltpu.VMEM((2 * width, width), BF16)] * 2
    if usual:
        far_b = jnp.concatenate([far_b, after(far_x, x1)], 0)
        got_far = swap(far_b, "tensor", 1)
        got_b = after(got_b, far_b)
    wide_per = 8 if rows % 8 == 0 else rows
    *first, keep_b, send_b = call(
        functools.partial(hidden_near_kernel, wide_per),
        "hidden_near",
        [(virt, smem), x1, cot, cot_t, vec, b, got_b],
        [
            pltpu.VMEM((own, width), BF16),
            pltpu.VMEM((own, width), F32),
            pltpu.VMEM((own, 1), F32),
            pltpu.VMEM((own, width), F32),
            pltpu.VMEM((own, width), F32),
            pltpu.VMEM((VDP, tall_b, width), F32),
            pltpu.VMEM((VDP, tall_b, width), BF16),
        ],
        [pltpu.VMEM((own, 2 * width), BF16)] * 2 + [pltpu.VMEM((width, own), BF16)] + mats,
        token_mm * 12 * width,
        12,
    )
    y, dx1, g, gout, gvec = call(
        functools.partial(hidden_far_kernel, wide_per),
        "hidden_far",
        [(virt, smem), cot, vec, far_b, got_far, *first, o],
        [
            pltpu.VMEM((own, width), BF16),
            pltpu.VMEM((own, width), F32),
            pltpu.VMEM((own, width), BF16),
            pltpu.VMEM((width, width), F32),
            pltpu.VMEM((8, width), F32),
        ],
        [pltpu.VMEM((width, own), BF16)] + mats,
        token_mm * 9 * width,
    )
    core, xbit, zlo = ("tensor", 1), ("dp", 1), ("dp", 2)
    if usual:
        held_b = fold_step(keep_b, send_b, *core, g)
        y = after(y, held_b)
    y_near = swap(y, "tensor", 1)
    dqkv, keep_a, send_a, sums = call(
        functools.partial(back_kernel, per),
        "back",
        [(virt, smem), qkv, prob, g, xhat_t, wqkv, wout, vec, gout, gvec],
        [
            pltpu.VMEM((own, 3 * width), BF16),
            pltpu.VMEM((VDP, 32, width), F32),
            pltpu.VMEM((VDP * 32 + 8, width), BF16),
            pltpu.VMEM((8, width), F32),
        ],
        [pltpu.VMEM((width, 3 * width), F32)],
        token_mm * (4 * width + 5 * WIN),
    )
    if usual:
        held_b = fold_step(*halves(held_b), *xbit)
        got = after(swap(send_a, *core), held_b).astype(F32)
        held_a = keep_a + got[:-8].reshape(keep_a.shape)
        sums = sums + got[-8:]
        vec = after(vec, held_a)
    gx, gxb, layer_out = call(
        functools.partial(token_grad_kernel, less),
        "token_grad",
        [(me, smem), dqkv, wqkv, vec, xhat1, inv1, dx1, y, y_near],
        [
            pltpu.VMEM((own, width), F32),
            pltpu.VMEM((own, width), BF16),
            struct((images * seq_len, width), BF16),
        ],
        [pltpu.VMEM((3 * width, width), BF16), pltpu.SemaphoreType.DMA((2,))],
        flops=token_mm * 3 * width,
    )
    layer_out = layer_out.reshape(images, seq_len, width)

    def place(gx_near):
        return call(
            functools.partial(place_kernel, less),
            "place",
            [(me, smem), gx, gx_near],
            [struct((images * seq_len, width), F32)],
            [pltpu.VMEM((own, width), F32), pltpu.SemaphoreType.DMA((rows // less + 1,))],
        )[0].reshape(images, seq_len, width)

    if usual:
        held_b = fold_step(*halves(held_b), *zlo, gxb)
        send_a = jnp.concatenate([held_a[4:].reshape(-1, width), sums], 0).astype(BF16)
        got = after(swap(send_a, *xbit), (gxb, held_b)).astype(F32)
        held_a = held_a[:4] + got[:-8].reshape(4, -1, width)
        sums = sums + got[-8:]
        got = [
            swap(jnp.concatenate([held_a[n], sums] + more, 0).astype(BF16), "dp", 2 * n)
            for n, more in ((1, []), (2, [held_b[1]]), (3, []))
        ]
        grad_tokens = place(swap(after(gxb, held_a), "tensor", 1))
        got[2] = after(got[2], grad_tokens)
        shapes = ((small, 3 * width), (small, width), (2, small), (3, small), (tall, width), (tall, width))
        o_qkv, o_out, o_gains, o_bias, o_up, o_down = call(
            finish_kernel,
            "finish",
            [(me, smem), held_a, held_b, sums, *got],
            [struct(shape, F32) for shape in shapes],
            limit=2,
            hbm_outs=False,
        )
    else:
        grad_tokens = place(swap(gxb, "tensor", 1))
        send_a = send_a[:-8].reshape(keep_a.shape)
        grad_a, grad_b = other_reduce((keep_a, send_a), (keep_b, send_b), sums, index, n_dp, n_t)
        o_qkv = jnp.concatenate([grad_a[p * small : (p + 1) * small] for p in range(3)], 1)
        o_out = grad_a[3 * small : 4 * small]
        o_vec = lax.dynamic_slice_in_dim(grad_a[4 * small : 4 * small + 5], index * small, small, 1)
        o_gains, o_bias = o_vec[:2], o_vec[2:]
        o_up, o_down = grad_b[:tall], grad_b[tall:]
    return layer_out, grad_tokens, o_qkv, o_out, o_gains, o_bias, o_up, o_down.T


def solution(mesh):
    in_specs = (
        P("dp", None, None),
        P("dp"),
        P("dp", None),
        P("dp", None, None),
        P(("dp", "tensor"), None),
        P(("dp", "tensor"), None),
        P(None, ("dp", "tensor")),
        P(None, ("dp", "tensor")),
        P("dp", "tensor"),
        P("tensor", "dp"),
    )
    out_specs = (
        P("dp", None, None),
        P("dp", None, None),
        P(("dp", "tensor"), None),
        P(("dp", "tensor"), None),
        P(None, ("dp", "tensor")),
        P(None, ("dp", "tensor")),
        P("dp", "tensor"),
        P("tensor", "dp"),
    )
    return jax.shard_map(
        on_device, mesh=mesh, in_specs=in_specs, out_specs=out_specs, check_vma=False
    )
```

profile of v0, /device:TPU:0, one launch (start us, length us, event | category | flops | bytes accessed | tf_op | source)
XLA Modules:
  0.0 58.3 jit_solution(14594939942217052327)
XLA Ops:
  0.6 0.9 %pack.1 = bf16[1,104,256]{2,1,0:T(8,128)(2,1)S(1)} custom-call(s32[1]{0:T(128)} %bitcast.me.virt, bf16[8,768]{1,0:T(8,128)(2,1)} %refs_0_.1, bf16[8,256]{1,0:T(8,128)(2,1)} %refs_1_.1, bf16[2,8]{1,0:T(2,128)(2,1)} %refs_2_.1, bf16[3,8]{1,0:T(4,128)(2,1)} %refs_3_.1, bf16[32,256]{1,0:T(8,128)(2,1)} %refs_4_.1, bf16[32,256]{1,0:T(8,128)(2,1)} %bitcast.55), custom_call_target="tpu_custom_call" | custom-call | bytes 49236 | tf_op jit(solution)/shard_map/pack/pallas_call | solution.py:547
  1.6 5.1 %collective-permute-start.2 = (bf16[1,104,256]{2,1,0:T(8,128)(2,1)S(1)}, bf16[1,104,256]{2,1,0:T(8,128)(2,1)S(1)}, u32[]{:S(2)}, u32[]{:S(2)}) collective-permute-start(bf16[1,104,256]{2,1,0:T(8,128)(2,1)S(1)} %pack.1), channel_id=1, source_target_pairs={{0,24},{4,28},{8,16},{12,20},{16,8},{20,12},{24,0},{28,4},{1,25},{... | collective-permute-start | bytes 159752 | tf_op jit(solution)/shard_map/ppermute | solution.py:421
  6.7 0.0 collective-permute-start.1
  6.7 0.6 %collective-permute-start = (bf16[1,104,256]{2,1,0:T(8,128)(2,1)S(1)}, bf16[1,104,256]{2,1,0:T(8,128)(2,1)S(1)}, u32[]{:S(2)}, u32[]{:S(2)}) collective-permute-start(bf16[1,104,256]{2,1,0:T(8,128)(2,1)S(1)} %pack.1), channel_id=1, source_target_pairs={{0,8},{4,12},{8,0},{12,4},{16,24},{20,28},{24,16},{28,20},{1,9},{5... | collective-permute-start | bytes 159752 | tf_op jit(solution)/shard_map/ppermute | solution.py:421
  7.4 1.7 %turn.1 = (bf16[2304,256]{1,0:T(8,128)(2,1)S(1)}, bf16[256,2304]{1,0:T(8,128)(2,1)S(1)}, bf16[2304,256]{1,0:T(8,128)(2,1)S(1)}) custom-call(s32[1]{0:T(128)} %bitcast.me.virt, bf16[4608,256]{1,0:T(8,128)(2,1)} %bitcast.50, bf16[4608,256]{1,0:T(8,128)(2,1)} %bitcast.51), custom_call_target="tpu_custom_call" | custom-call | bytes 4718596 | tf_op jit(solution)/shard_map/turn/pallas_call | solution.py:547
  9.0 1.8 %collective-permute-done = bf16[1,104,256]{2,1,0:T(8,128)(2,1)S(1)} collective-permute-done((bf16[1,104,256]{2,1,0:T(8,128)(2,1)S(1)}, bf16[1,104,256]{2,1,0:T(8,128)(2,1)S(1)}, u32[]{:S(2)}, u32[]{:S(2)}) %collective-permute-start) | collective-permute-done | bytes 53280 | tf_op jit(solution)/shard_map/ppermute | solution.py:421
  10.9 0.0 collective-permute-done.2
  10.9 0.9 %collective-permute-done.1 = bf16[1,104,256]{2,1,0:T(8,128)(2,1)S(1)} collective-permute-done((bf16[1,104,256]{2,1,0:T(8,128)(2,1)S(1)}, bf16[1,104,256]{2,1,0:T(8,128)(2,1)S(1)}, u32[]{:S(2)}, u32[]{:S(2)}) %collective-permute-start.1) | collective-permute-done | bytes 53280 | tf_op jit(solution)/shard_map/ppermute | solution.py:421
  11.8 0.0 copy-start
  11.8 0.0 copy-start.1
  11.8 1.6 %collective-permute-start.3 = (bf16[136,256]{1,0:T(8,128)(2,1)S(1)}, bf16[136,256]{1,0:T(8,128)(2,1)S(1)}, u32[]{:S(2)}, u32[]{:S(2)}) collective-permute-start(bf16[136,256]{1,0:T(8,128)(2,1)S(1)} %get-tuple-element.116), channel_id=1, source_target_pairs={{0,4},{4,0},{8,12},{12,8},{16,20},{20,16},{24,28},{28,24},{1,5},{5... | collective-permute-start | bytes 208904 | tf_op jit(solution)/shard_map/ppermute | solution.py:421
  13.4 0.6 %collective-permute-start.6 = (bf16[4,64,256]{2,1,0:T(8,128)(2,1)S(1)}, bf16[4,64,256]{2,1,0:T(8,128)(2,1)S(1)}, u32[]{:S(2)}, u32[]{:S(2)}) collective-permute-start(bf16[4,64,256]{2,1,0:T(8,128)(2,1)S(1)} %pad_maximum_fusion), channel_id=1, source_target_pairs={{0,4},{4,0},{8,12},{12,8},{16,20},{20,16},{24,28},{28,24},{1,5},{5... | collective-permute-start | bytes 393224 | tf_op jit(solution)/shard_map/ppermute | solution.py:421
  14.0 1.5 %collective-permute-start.4 = (bf16[4,64,256]{2,1,0:T(8,128)(2,1)S(1)}, bf16[4,64,256]{2,1,0:T(8,128)(2,1)S(1)}, u32[]{:S(2)}, u32[]{:S(2)}) collective-permute-start(bf16[4,64,256]{2,1,0:T(8,128)(2,1)S(1)} %pad_maximum_fusion), channel_id=1, source_target_pairs={{0,2},{1,3},{2,0},{3,1},{4,6},{5,7},{6,4},{7,5},{8,10},{9,11},{10,... | collective-permute-start | bytes 393224 | tf_op jit(solution)/shard_map/ppermute | solution.py:421
  15.5 1.4 %collective-permute-done.3 = bf16[136,256]{1,0:T(8,128)(2,1)S(1)} collective-permute-done((bf16[136,256]{1,0:T(8,128)(2,1)S(1)}, bf16[136,256]{1,0:T(8,128)(2,1)S(1)}, u32[]{:S(2)}, u32[]{:S(2)}) %collective-permute-start.3) | collective-permute-done | bytes 69664 | tf_op jit(solution)/shard_map/ppermute | solution.py:421
  16.9 1.6 %collective-permute-start.5 = (bf16[264,256]{1,0:T(8,128)(2,1)S(1)}, bf16[264,256]{1,0:T(8,128)(2,1)S(1)}, u32[]{:S(2)}, u32[]{:S(2)}) collective-permute-start(bf16[264,256]{1,0:T(8,128)(2,1)S(1)} %constant_dynamic-update-slice_fusion.5), channel_id=1, source_target_pairs={{0,2},{1,3},{2,0},{3,1},{4,6},{5,7},{6,4},{7,5},{8,10},{9,11},{10,... | collective-permute-start | bytes 405512 | tf_op jit(solution)/shard_map/ppermute | solution.py:421
  18.5 1.1 %collective-permute-done.4 = bf16[4,64,256]{2,1,0:T(8,128)(2,1)S(1)} collective-permute-done((bf16[4,64,256]{2,1,0:T(8,128)(2,1)S(1)}, bf16[4,64,256]{2,1,0:T(8,128)(2,1)S(1)}, u32[]{:S(2)}, u32[]{:S(2)}) %collective-permute-start.4) | collective-permute-done | bytes 131104 | tf_op jit(solution)/shard_map/ppermute | solution.py:421
  19.6 1.0 %first_norm.1 = (f32[2304,256]{1,0:T(8,128)S(1)}, f32[2304,1]{1,0:T(8,128)S(1)}, bf16[272,2304]{1,0:T(8,128)(2,1)S(1)}) custom-call(bf16[2304,256]{1,0:T(8,128)(2,1)S(1)} %get-tuple-element.64.x_ref), custom_call_target="tpu_custom_call" | custom-call | bytes 1179648 | tf_op jit(solution)/shard_map/first_norm/pallas_call | solution.py:547
  20.6 0.0 collective-permute-done.6
  20.6 1.4 %collective-permute-done.5 = bf16[264,256]{1,0:T(8,128)(2,1)S(1)} collective-permute-done((bf16[264,256]{1,0:T(8,128)(2,1)S(1)}, bf16[264,256]{1,0:T(8,128)(2,1)S(1)}, u32[]{:S(2)}, u32[]{:S(2)}) %collective-permute-start.5) | collective-permute-done | bytes 135200 | tf_op jit(solution)/shard_map/ppermute | solution.py:421
  22.0 0.1 collective-permute-start.7
  22.1 0.5 collective-permute-start.10
  22.6 1.0 %collective-permute-start.8 = (bf16[4,64,256]{2,1,0:T(8,128)(2,1)S(1)}, bf16[4,64,256]{2,1,0:T(8,128)(2,1)S(1)}, u32[]{:S(2)}, u32[]{:S(2)}) collective-permute-start(bf16[4,64,256]{2,1,0:T(8,128)(2,1)S(1)} %collective-permute-done.4), channel_id=1, source_target_pairs={{0,4},{4,0},{8,12},{12,8},{16,20},{20,16},{24,28},{28,24},{1,5},{5... | collective-permute-start | bytes 393224 | tf_op jit(solution)/shard_map/ppermute | solution.py:421
  23.6 0.1 collective-permute-done.7.got
  23.7 0.0 copy-done
  23.7 0.0 copy-done.1
  23.7 3.6 %attend.1 = (bf16[2304,768]{1,0:T(8,128)(2,1)S(1)}, bf16[24,96,256]{2,1,0:T(8,128)(2,1)S(1)}, bf16[2304,256]{1,0:T(8,128)(2,1)S(1)}, f32[2304,256]{1,0:T(8,128)S...) custom-call(s32[1]{0:T(128)} %bitcast.me.virt, s32[1]{0:T(128)} %bitcast.me.virt, ...), custom_call_target="tpu_custom_call" | custom-call | flops 1434451968 | bytes 4071640 | tf_op jit(solution)/shard_map/attend/pallas_call | solution.py:547
  27.3 0.8 %collective-permute-done.8 = bf16[4,64,256]{2,1,0:T(8,128)(2,1)S(1)} collective-permute-done((bf16[4,64,256]{2,1,0:T(8,128)(2,1)S(1)}, bf16[4,64,256]{2,1,0:T(8,128)(2,1)S(1)}, u32[]{:S(2)}, u32[]{:S(2)}) %collective-permute-start.8) | collective-permute-done | bytes 131104 | tf_op jit(solution)/shard_map/ppermute | solution.py:421
  28.1 0.1 collective-permute-start.9
  28.2 0.0 collective-permute-done.10.got
  28.2 4.9 %hidden_near.1 = (bf16[2304,256]{1,0:T(8,128)(2,1)S(1)}, f32[2304,256]{1,0:T(8,128)S(1)}, f32[2304,1]{1,0:T(8,128)S(1)}, f32[2304,256]{1,0:T(8,128)S(1)}, f32[23...) custom-call(s32[1]{0:T(128)} %bitcast.me.virt, ...), custom_call_target="tpu_custom_call" | custom-call | flops 3623878656 | bytes 5251076 | tf_op jit(solution)/shard_map/hidden_near/pallas_call | solution.py:547
  33.1 0.5 collective-permute-start.12
  33.6 0.0 collective-permute-done.9.got
  33.6 4.5 %hidden_far.1 = (bf16[2304,256]{1,0:T(8,128)(2,1)S(1)}, f32[2304,256]{1,0:T(8,128)S(1)}, bf16[2304,256]{1,0:T(8,128)(2,1)S(1)}, f32[256,256]{1,0:T(8,128)S(1)}, f32[8,256]{1,0:T(8,128)S(1)}) custom-call(s32[1]{0:T(128)} %bitcast.me.virt, bf16[2304,256]{1,0:T(8,128)(2,1)S(1)} %get-tuple-element.62.cot_ref, f32[8,256]{1,0:T(8,128)S(1)} %get-tuple-element.93.vec, ...), custom_call_target="tpu_custom_call" | custom-call | flops 2717908992 | bytes 11158532 | tf_op jit(solution)/shard_map/hidden_far/pallas_call | solution.py:547
  38.2 0.0 collective-permute-done.12
  38.2 0.1 convert_add_fusion
  38.3 0.1 collective-permute-start.14
  38.4 1.0 %collective-permute-start.13 = (bf16[4,64,256]{2,1,0:T(8,128)(2,1)S(1)}, bf16[4,64,256]{2,1,0:T(8,128)(2,1)S(1)}, u32[]{:S(2)}, u32[]{:S(2)}) collective-permute-start(bf16[4,64,256]{2,1,0:T(8,128)(2,1)S(1)} %slice.253), channel_id=1, source_target_pairs={{0,4},{4,0},{8,12},{12,8},{16,20},{20,16},{24,28},{28,24},{1,5},{5... | collective-permute-start | bytes 393224 | tf_op jit(solution)/shard_map/ppermute | solution.py:421
  39.4 4.0 %back.1 = (bf16[2304,768]{1,0:T(8,128)(2,1)S(1)}, f32[8,32,256]{2,1,0:T(8,128)S(1)}, bf16[264,256]{1,0:T(8,128)(2,1)S(1)}, f32[8,256]{1,0:T(8,128)S(1)}) custom-call(s32[1]{0:T(128)} %bitcast.me.virt, bf16[2304,768]{1,0:T(8,128)(2,1)S(1)} %get-tuple-element.67.qkv_ref, bf16[24,96,256]{2,1,0:T(8,128)(2,1)S(1)} %get-tuple-element.68.prob_ref, ...), custom_call_target="tpu_custom_call" | custom-call | flops 1774190592 | bytes 7954436 | tf_op jit(solution)/shard_map/back/pallas_call | solution.py:547
  43.4 0.3 collective-permute-start.11
  43.6 0.7 %collective-permute-done.13 = bf16[4,64,256]{2,1,0:T(8,128)(2,1)S(1)} collective-permute-done((bf16[4,64,256]{2,1,0:T(8,128)(2,1)S(1)}, bf16[4,64,256]{2,1,0:T(8,128)(2,1)S(1)}, u32[]{:S(2)}, u32[]{:S(2)}) %collective-permute-start.13) | collective-permute-done | bytes 131104 | tf_op jit(solution)/shard_map/ppermute | solution.py:421
  44.4 0.8 %collective-permute-start.16 = (bf16[2,64,256]{2,1,0:T(8,128)(2,1)S(1)}, bf16[2,64,256]{2,1,0:T(8,128)(2,1)S(1)}, u32[]{:S(2)}, u32[]{:S(2)}) collective-permute-start(bf16[2,64,256]{2,1,0:T(8,128)(2,1)S(1)} %slice.254), channel_id=1, source_target_pairs={{0,8},{4,12},{8,0},{12,4},{16,24},{20,28},{24,16},{28,20},{1,9},{5... | collective-permute-start | bytes 196616 | tf_op jit(solution)/shard_map/ppermute | solution.py:421
  45.2 0.0 collective-permute-done.11
  45.3 1.0 %collective-permute-start.15 = (bf16[136,256]{1,0:T(8,128)(2,1)S(1)}, bf16[136,256]{1,0:T(8,128)(2,1)S(1)}, u32[]{:S(2)}, u32[]{:S(2)}) collective-permute-start(bf16[136,256]{1,0:T(8,128)(2,1)S(1)} %pad_maximum_fusion.1), channel_id=1, source_target_pairs={{0,4},{4,0},{8,12},{12,8},{16,20},{20,16},{24,28},{28,24},{1,5},{5... | collective-permute-start | bytes 208904 | tf_op jit(solution)/shard_map/ppermute | solution.py:421
  46.4 0.0 collective-permute-done.14.y_near
  46.4 1.8 %token_grad.1 = (f32[2304,256]{1,0:T(8,128)S(1)}, bf16[2304,256]{1,0:T(8,128)(2,1)S(1)}, bf16[4608,256]{1,0:T(8,128)(2,1)}) custom-call(s32[1]{0:T(128)} %bitcast.me.virt, bf16[2304,768]{1,0:T(8,128)(2,1)S(1)} %get-tuple-element.86.dqkv, bf16[256,768]{1,0:T(8,128)(2,1)S(1)} %get-tuple-element.82.wqkv, f32[8,256]{1,0:T(8,128)S(1)} %get-tuple-element.93.vec, ...), custom_call_target="tpu_custom_call" | custom-call | flops 905969664 | bytes 11027460 | tf_op jit(solution)/shard_map/token_grad/pallas_call | solution.py:547
  48.1 0.6 collective-permute-done.16
  48.7 1.0 %collective-permute-done.15 = bf16[136,256]{1,0:T(8,128)(2,1)S(1)} collective-permute-done((bf16[136,256]{1,0:T(8,128)(2,1)S(1)}, bf16[136,256]{1,0:T(8,128)(2,1)S(1)}, u32[]{:S(2)}, u32[]{:S(2)}) %collective-permute-start.15) | collective-permute-done | bytes 69664 | tf_op jit(solution)/shard_map/ppermute | solution.py:421
  49.7 0.1 collective-permute-start.17
  49.9 1.9 %collective-permute-start.19 = (bf16[104,256]{1,0:T(8,128)(2,1)S(1)}, bf16[104,256]{1,0:T(8,128)(2,1)S(1)}, u32[]{:S(2)}, u32[]{:S(2)}) collective-permute-start(bf16[104,256]{1,0:T(8,128)(2,1)S(1)} %pad_maximum_fusion.2), channel_id=1, source_target_pairs={{0,16},{4,20},{8,24},{12,28},{16,0},{20,4},{24,8},{28,12},{1,17},{... | collective-permute-start | bytes 159752 | tf_op jit(solution)/shard_map/ppermute | solution.py:421
  51.8 1.8 %collective-permute-start.20 = (bf16[40,256]{1,0:T(8,128)(2,1)S(1)}, bf16[40,256]{1,0:T(8,128)(2,1)S(1)}, u32[]{:S(2)}, u32[]{:S(2)}) collective-permute-start(bf16[40,256]{1,0:T(8,128)(2,1)S(1)} %get-tuple-element.143), channel_id=1, source_target_pairs={{0,24},{4,28},{8,16},{12,20},{16,8},{20,12},{24,0},{28,4},{1,25},{... | collective-permute-start | bytes 61448 | tf_op jit(solution)/shard_map/ppermute | solution.py:421
  53.6 0.0 collective-permute-start.18
  53.6 0.0 collective-permute-done.17.theirs
  53.6 2.2 %place.1 = f32[4608,256]{1,0:T(8,128)} custom-call(s32[1]{0:T(128)} %bitcast.me.virt, f32[2304,256]{1,0:T(8,128)S(1)} %get-tuple-element.99.mine, bf16[2304,256]{1,0:T(8,128)(2,1)S(1)} %collective-permute-done.17.theirs), custom_call_target="tpu_custom_call" | custom-call | bytes 3538948 | tf_op jit(solution)/shard_map/place/pallas_call | solution.py:547
  55.9 1.5 %collective-permute-done.20.refs_2_ = bf16[40,256]{1,0:T(8,128)(2,1)S(1)} collective-permute-done((bf16[40,256]{1,0:T(8,128)(2,1)S(1)}, bf16[40,256]{1,0:T(8,128)(2,1)S(1)}, u32[]{:S(2)}, u32[]{:S(2)}) %collective-permute-start.20) | collective-permute-done | bytes 20512 | tf_op jit(solution)/shard_map/ppermute | solution.py:421
  57.4 0.2 collective-permute-done.18.refs_0_
  57.6 0.0 collective-permute-done.19.refs_1_
  57.6 0.7 %finish.1 = (f32[8,768]{1,0:T(8,128)}, f32[8,256]{1,0:T(8,128)}, f32[2,8]{1,0:T(2,128)}, f32[3,8]{1,0:T(4,128)}, f32[32,256]{1,0:T(8,128)}, /*index=5*/f32[32,256]{1,0:T(8,128)}) custom-call(s32[1]{0:T(128)} %bitcast.me.virt, f32[4,32,256]{2,1,0:T(8,128)S(1)} %get-tuple-element.113.keep_a, f32[2,64,256]{2,1,0:T(8,128)S(1)} %slice_add_fusion.1.keep_b, ...), custom_call_target="tpu_custom_call" | custom-call | bytes 364548 | tf_op jit(solution)/shard_map/finish/pallas_call | solution.py:547
  (35 shorter events, 0.4 us)
Async XLA Ops:
  1.6 9.3 %collective-permute-start.2 = (bf16[1,104,256]{2,1,0:T(8,128)(2,1)S(1)}, bf16[1,104,256]{2,1,0:T(8,128)(2,1)S(1)}, u32[]{:S(2)}, u32[]{:S(2)}) collective-permute-start(bf16[1,104,256]{2,1,0:T(8,128)(2,1)S(1)} %pack.1), channel_id=1, source_target_pairs={{0,24},{4,28},{8,16},{12,20},{16,8},{20,12},{24,0},{28,4},{1,25},{... | collective-permute-start | bytes 159752 | tf_op jit(solution)/shard_map/ppermute | solution.py:421
  6.7 5.0 %collective-permute-start.1 = (bf16[1,104,256]{2,1,0:T(8,128)(2,1)S(1)}, bf16[1,104,256]{2,1,0:T(8,128)(2,1)S(1)}, u32[]{:S(2)}, u32[]{:S(2)}) collective-permute-start(bf16[1,104,256]{2,1,0:T(8,128)(2,1)S(1)} %pack.1), channel_id=1, source_target_pairs={{0,16},{4,20},{8,24},{12,28},{16,0},{20,4},{24,8},{28,12},{1,17},{... | collective-permute-start | bytes 159752 | tf_op jit(solution)/shard_map/ppermute | solution.py:421
  6.7 4.1 %collective-permute-start = (bf16[1,104,256]{2,1,0:T(8,128)(2,1)S(1)}, bf16[1,104,256]{2,1,0:T(8,128)(2,1)S(1)}, u32[]{:S(2)}, u32[]{:S(2)}) collective-permute-start(bf16[1,104,256]{2,1,0:T(8,128)(2,1)S(1)} %pack.1), channel_id=1, source_target_pairs={{0,8},{4,12},{8,0},{12,4},{16,24},{20,28},{24,16},{28,20},{1,9},{5... | collective-permute-start | bytes 159752 | tf_op jit(solution)/shard_map/ppermute | solution.py:421
  11.8 11.9 %copy-start = (s32[4,12]{1,0:T(4,128)S(1)}, s32[4,12]{1,0:T(4,128)}, u32[]{:S(2)}) copy-start(s32[4,12]{1,0:T(4,128)} %live.1) | copy-start | bytes 580
  11.8 11.8 %copy-start.1 = (s32[4]{0:T(128)S(1)}, s32[4]{0:T(128)}, u32[]{:S(2)}) copy-start(s32[4]{0:T(128)} %lens.1) | copy-start | bytes 52
  11.8 5.1 %collective-permute-start.3 = (bf16[136,256]{1,0:T(8,128)(2,1)S(1)}, bf16[136,256]{1,0:T(8,128)(2,1)S(1)}, u32[]{:S(2)}, u32[]{:S(2)}) collective-permute-start(bf16[136,256]{1,0:T(8,128)(2,1)S(1)} %get-tuple-element.116), channel_id=1, source_target_pairs={{0,4},{4,0},{8,12},{12,8},{16,20},{20,16},{24,28},{28,24},{1,5},{5... | collective-permute-start | bytes 208904 | tf_op jit(solution)/shard_map/ppermute | solution.py:421
  13.4 7.2 %collective-permute-start.6 = (bf16[4,64,256]{2,1,0:T(8,128)(2,1)S(1)}, bf16[4,64,256]{2,1,0:T(8,128)(2,1)S(1)}, u32[]{:S(2)}, u32[]{:S(2)}) collective-permute-start(bf16[4,64,256]{2,1,0:T(8,128)(2,1)S(1)} %pad_maximum_fusion), channel_id=1, source_target_pairs={{0,4},{4,0},{8,12},{12,8},{16,20},{20,16},{24,28},{28,24},{1,5},{5... | collective-permute-start | bytes 393224 | tf_op jit(solution)/shard_map/ppermute | solution.py:421
  14.0 5.6 %collective-permute-start.4 = (bf16[4,64,256]{2,1,0:T(8,128)(2,1)S(1)}, bf16[4,64,256]{2,1,0:T(8,128)(2,1)S(1)}, u32[]{:S(2)}, u32[]{:S(2)}) collective-permute-start(bf16[4,64,256]{2,1,0:T(8,128)(2,1)S(1)} %pad_maximum_fusion), channel_id=1, source_target_pairs={{0,2},{1,3},{2,0},{3,1},{4,6},{5,7},{6,4},{7,5},{8,10},{9,11},{10,... | collective-permute-start | bytes 393224 | tf_op jit(solution)/shard_map/ppermute | solution.py:421
  16.9 5.1 %collective-permute-start.5 = (bf16[264,256]{1,0:T(8,128)(2,1)S(1)}, bf16[264,256]{1,0:T(8,128)(2,1)S(1)}, u32[]{:S(2)}, u32[]{:S(2)}) collective-permute-start(bf16[264,256]{1,0:T(8,128)(2,1)S(1)} %constant_dynamic-update-slice_fusion.5), channel_id=1, source_target_pairs={{0,2},{1,3},{2,0},{3,1},{4,6},{5,7},{6,4},{7,5},{8,10},{9,11},{10,... | collective-permute-start | bytes 405512 | tf_op jit(solution)/shard_map/ppermute | solution.py:421
  22.0 1.6 %collective-permute-start.7 = (bf16[520,256]{1,0:T(8,128)(2,1)S(1)}, bf16[520,256]{1,0:T(8,128)(2,1)S(1)}, u32[]{:S(2)}, u32[]{:S(2)}) collective-permute-start(bf16[520,256]{1,0:T(8,128)(2,1)S(1)} %constant_dynamic-update-slice_fusion.15.held), channel_id=1, source_target_pairs={{0,1},{1,0},{2,3},{3,2},{4,5},{5,4},{6,7},{7,6},{8,9},{9,8},{10,11... | collective-permute-start | bytes 798728 | tf_op jit(solution)/shard_map/ppermute | solution.py:421
  22.1 6.1 %collective-permute-start.10 = (bf16[8,64,256]{2,1,0:T(8,128)(2,1)S(1)}, bf16[8,64,256]{2,1,0:T(8,128)(2,1)S(1)}, u32[]{:S(2)}, u32[]{:S(2)}) collective-permute-start(bf16[8,64,256]{2,1,0:T(8,128)(2,1)S(1)} %constant_dynamic-update-slice_fusion.10.own), channel_id=1, source_target_pairs={{0,1},{1,0},{2,3},{3,2},{4,5},{5,4},{6,7},{7,6},{8,9},{9,8},{10,11... | collective-permute-start | bytes 786440 | tf_op jit(solution)/shard_map/ppermute | solution.py:421
  22.6 5.5 %collective-permute-start.8 = (bf16[4,64,256]{2,1,0:T(8,128)(2,1)S(1)}, bf16[4,64,256]{2,1,0:T(8,128)(2,1)S(1)}, u32[]{:S(2)}, u32[]{:S(2)}) collective-permute-start(bf16[4,64,256]{2,1,0:T(8,128)(2,1)S(1)} %collective-permute-done.4), channel_id=1, source_target_pairs={{0,4},{4,0},{8,12},{12,8},{16,20},{20,16},{24,28},{28,24},{1,5},{5... | collective-permute-start | bytes 393224 | tf_op jit(solution)/shard_map/ppermute | solution.py:421
  28.1 5.5 %collective-permute-start.9 = (bf16[8,64,256]{2,1,0:T(8,128)(2,1)S(1)}, bf16[8,64,256]{2,1,0:T(8,128)(2,1)S(1)}, u32[]{:S(2)}, u32[]{:S(2)}) collective-permute-start(bf16[8,64,256]{2,1,0:T(8,128)(2,1)S(1)} %constant_dynamic-update-slice_fusion.20.own), channel_id=1, source_target_pairs={{0,1},{1,0},{2,3},{3,2},{4,5},{5,4},{6,7},{7,6},{8,9},{9,8},{10,11... | collective-permute-start | bytes 786440 | tf_op jit(solution)/shard_map/ppermute | solution.py:421
  33.1 5.1 %collective-permute-start.12 = (bf16[8,64,256]{2,1,0:T(8,128)(2,1)S(1)}, bf16[8,64,256]{2,1,0:T(8,128)(2,1)S(1)}, u32[]{:S(2)}, u32[]{:S(2)}) collective-permute-start(bf16[8,64,256]{2,1,0:T(8,128)(2,1)S(1)} %get-tuple-element.90), channel_id=1, source_target_pairs={{0,1},{1,0},{2,3},{3,2},{4,5},{5,4},{6,7},{7,6},{8,9},{9,8},{10,11... | collective-permute-start | bytes 786440 | tf_op jit(solution)/shard_map/ppermute | solution.py:421
  38.3 8.1 %collective-permute-start.14 = (bf16[2304,256]{1,0:T(8,128)(2,1)S(1)}, bf16[2304,256]{1,0:T(8,128)(2,1)S(1)}, u32[]{:S(2)}, u32[]{:S(2)}) collective-permute-start(bf16[2304,256]{1,0:T(8,128)(2,1)S(1)} %get-tuple-element.97.y), channel_id=1, source_target_pairs={{0,1},{1,0},{2,3},{3,2},{4,5},{5,4},{6,7},{7,6},{8,9},{9,8},{10,11... | collective-permute-start | bytes 3538952 | tf_op jit(solution)/shard_map/ppermute | solution.py:421
  38.4 5.9 %collective-permute-start.13 = (bf16[4,64,256]{2,1,0:T(8,128)(2,1)S(1)}, bf16[4,64,256]{2,1,0:T(8,128)(2,1)S(1)}, u32[]{:S(2)}, u32[]{:S(2)}) collective-permute-start(bf16[4,64,256]{2,1,0:T(8,128)(2,1)S(1)} %slice.253), channel_id=1, source_target_pairs={{0,4},{4,0},{8,12},{12,8},{16,20},{20,16},{24,28},{28,24},{1,5},{5... | collective-permute-start | bytes 393224 | tf_op jit(solution)/shard_map/ppermute | solution.py:421
  43.4 1.8 %collective-permute-start.11 = (bf16[264,256]{1,0:T(8,128)(2,1)S(1)}, bf16[264,256]{1,0:T(8,128)(2,1)S(1)}, u32[]{:S(2)}, u32[]{:S(2)}) collective-permute-start(bf16[264,256]{1,0:T(8,128)(2,1)S(1)} %get-tuple-element.88), channel_id=1, source_target_pairs={{0,1},{1,0},{2,3},{3,2},{4,5},{5,4},{6,7},{7,6},{8,9},{9,8},{10,11... | collective-permute-start | bytes 405512 | tf_op jit(solution)/shard_map/ppermute | solution.py:421
  44.4 4.3 %collective-permute-start.16 = (bf16[2,64,256]{2,1,0:T(8,128)(2,1)S(1)}, bf16[2,64,256]{2,1,0:T(8,128)(2,1)S(1)}, u32[]{:S(2)}, u32[]{:S(2)}) collective-permute-start(bf16[2,64,256]{2,1,0:T(8,128)(2,1)S(1)} %slice.254), channel_id=1, source_target_pairs={{0,8},{4,12},{8,0},{12,4},{16,24},{20,28},{24,16},{28,20},{1,9},{5... | collective-permute-start | bytes 196616 | tf_op jit(solution)/shard_map/ppermute | solution.py:421
  45.3 4.4 %collective-permute-start.15 = (bf16[136,256]{1,0:T(8,128)(2,1)S(1)}, bf16[136,256]{1,0:T(8,128)(2,1)S(1)}, u32[]{:S(2)}, u32[]{:S(2)}) collective-permute-start(bf16[136,256]{1,0:T(8,128)(2,1)S(1)} %pad_maximum_fusion.1), channel_id=1, source_target_pairs={{0,4},{4,0},{8,12},{12,8},{16,20},{20,16},{24,28},{28,24},{1,5},{5... | collective-permute-start | bytes 208904 | tf_op jit(solution)/shard_map/ppermute | solution.py:421
  49.7 3.9 %collective-permute-start.17 = (bf16[2304,256]{1,0:T(8,128)(2,1)S(1)}, bf16[2304,256]{1,0:T(8,128)(2,1)S(1)}, u32[]{:S(2)}, u32[]{:S(2)}) collective-permute-start(bf16[2304,256]{1,0:T(8,128)(2,1)S(1)} %get-tuple-element.104), channel_id=1, source_target_pairs={{0,1},{1,0},{2,3},{3,2},{4,5},{5,4},{6,7},{7,6},{8,9},{9,8},{10,11... | collective-permute-start | bytes 3538952 | tf_op jit(solution)/shard_map/ppermute | solution.py:421
  49.9 7.7 %collective-permute-start.19 = (bf16[104,256]{1,0:T(8,128)(2,1)S(1)}, bf16[104,256]{1,0:T(8,128)(2,1)S(1)}, u32[]{:S(2)}, u32[]{:S(2)}) collective-permute-start(bf16[104,256]{1,0:T(8,128)(2,1)S(1)} %pad_maximum_fusion.2), channel_id=1, source_target_pairs={{0,16},{4,20},{8,24},{12,28},{16,0},{20,4},{24,8},{28,12},{1,17},{... | collective-permute-start | bytes 159752 | tf_op jit(solution)/shard_map/ppermute | solution.py:421
  51.8 5.6 %collective-permute-start.20 = (bf16[40,256]{1,0:T(8,128)(2,1)S(1)}, bf16[40,256]{1,0:T(8,128)(2,1)S(1)}, u32[]{:S(2)}, u32[]{:S(2)}) collective-permute-start(bf16[40,256]{1,0:T(8,128)(2,1)S(1)} %get-tuple-element.143), channel_id=1, source_target_pairs={{0,24},{4,28},{8,16},{12,20},{16,8},{20,12},{24,0},{28,4},{1,25},{... | collective-permute-start | bytes 61448 | tf_op jit(solution)/shard_map/ppermute | solution.py:421
  53.6 4.0 %collective-permute-start.18 = (bf16[40,256]{1,0:T(8,128)(2,1)S(1)}, bf16[40,256]{1,0:T(8,128)(2,1)S(1)}, u32[]{:S(2)}, u32[]{:S(2)}) collective-permute-start(bf16[40,256]{1,0:T(8,128)(2,1)S(1)} %get-tuple-element.144), channel_id=1, source_target_pairs={{0,8},{4,12},{8,0},{12,4},{16,24},{20,28},{24,16},{28,20},{1,9},{5... | collective-permute-start | bytes 61448 | tf_op jit(solution)/shard_map/ppermute | solution.py:421
where the time goes:
time: 58.6 us; the launch traced here: 58.3 us
  Pallas kernels  25.3 us (43%)
  starting transfers between devices  20.2 us (34%)
  waiting for transfers between devices  11.4 us (19%)
  between operations  0.97 us (2%)
    pallas_call x10, Pallas kernels, call(): pl.pallas_call(kernel, name=name, out_shape=outs, in_specs=[pl.BlockSpec(...  25.3 us
    ppermute x21, starting transfers between devices, swap(): return lax.ppermute(block, axis, [(i, i ^ bit) for i in range(size)])  20.2 us
    ppermute x21, waiting for transfers between devices, swap(): return lax.ppermute(block, axis, [(i, i ^ bit) for i in range(size)])  11.4 us
  transfers between devices with their start and end apart: 21, of which 12 were waited for; matrix products, arithmetic and copies ran while one was open for 1% of the time, Pallas kernels for 41%

commit v1 on v0

--- a/solution.py
+++ b/solution.py
@@ -212,11 +212,12 @@
         down_t[at, cols] = blocks[k, tall:]
 
 
-def hidden_units(h2, dyb, up, down_t):
+def hidden_units(h2, dyb, up, down_t, between=None):
     u = dot(h2, up[...], NN).astype(BF16)
     da = dot(dyb, down_t[...], NN).astype(BF16)
+    done = between() if between is not None else None
     a, slope = gelu_both(u)
-    return a, da * slope
+    return a, da * slope, done
 
 
 def hidden_near_kernel(
@@ -230,19 +231,26 @@
     join(virt, got, 1, up, down_t)
     up_t[...] = up[...].T
     down[...] = down_t[...].T
-    for c in range(tokens // size):
+    count = tokens // size
+
+    def norm(c):
         part = slice(c * size, (c + 1) * size)
-        x1 = x1_ref[part]
-        xhat, inv = norm_parts(x1)
+        xhat, inv = norm_parts(x1_ref[part])
         xhat_ref[part] = xhat
         inv_ref[part] = inv
         h2 = (xhat * vec[1:2] + vec[3:4]).astype(BF16)
         h2_ref[part] = h2
         h2_t[:, part] = h2.T
-        a, du = hidden_units(h2, cot_ref[part], up, down_t)
+        return h2
+
+    h2 = norm(0)
+    for c in range(count):
+        part = slice(c * size, (c + 1) * size)
+        later = functools.partial(norm, c + 1) if c + 1 < count else None
+        a, du, h2 = hidden_units(h2, cot_ref[part], up, down_t, later)
         a_ref[part] = a
         du_ref[part] = du
-        f_ref[part] = x1 + vec[4:5] + dot(a, down[...], NN)
+        f_ref[part] = x1_ref[part] + vec[4:5] + dot(a, down[...], NN)
         dh2_ref[part] = dot(du, up_t[...], NN)
     gdown = dot(cot_t[...], a_ref[...], NN)
     gup = dot(h2_t[...], du_ref[...], NN)
@@ -269,12 +277,21 @@
     up_t[...] = up[...].T
     down[...] = down_t[...].T
     sums = [jnp.zeros((1, width), F32)] * 3
-    for c in range(tokens // size):
+    count = tokens // size
+
+    def units(c):
         part = slice(c * size, (c + 1) * size)
         o_t[:, part] = o_ref[part].T
-        a, du = hidden_units(h2_ref[part], cot_ref[part], up, down_t)
+        return hidden_units(h2_ref[part], cot_ref[part], up, down_t)[:2]
+
+    ahead = units(0)
+    for c in range(count):
+        part = slice(c * size, (c + 1) * size)
+        a, du = ahead
         y_ref[part] = (f_ref[part] + dot(a, down[...], NN)).astype(BF16)
         dh2 = dh2_ref[part] + dot(du, up_t[...], NN)
+        if c + 1 < count:
+            ahead = units(c + 1)
         dy = cot_ref[part].astype(F32)
         xhat = xhat_ref[part]
         dx1 = dy + norm_back(dh2, xhat, inv_ref[part], vec[1:2])

time: 58.6 us -> 58.6 us (level)
  no operation moved by 1% of the time
where the time goes in v1:
time: 58.6 us; the launch traced here: 58.3 us
  Pallas kernels  25.3 us (43%)
  starting transfers between devices  20.2 us (34%)
  waiting for transfers between devices  11.4 us (19%)
  between operations  0.97 us (2%)
    pallas_call x10, Pallas kernels, call(): pl.pallas_call(kernel, name=name, out_shape=outs, in_specs=[pl.BlockSpec(...  25.3 us
    ppermute x21, starting transfers between devices, swap(): return lax.ppermute(block, axis, [(i, i ^ bit) for i in range(size)])  20.2 us
    ppermute x21, waiting for transfers between devices, swap(): return lax.ppermute(block, axis, [(i, i ^ bit) for i in range(size)])  11.4 us
  transfers between devices with their start and end apart: 21, of which 12 were waited for; matrix products, arithmetic and copies ran while one was open for 1% of the time, Pallas kernels for 41%

profile of v1, /device:TPU:0, one launch (start us, length us, event | category | flops | bytes accessed | tf_op | source)
XLA Modules:
  0.0 58.3 jit_solution(7638295135080658890)
XLA Ops:
  0.6 0.9 %pack.1 = bf16[1,104,256]{2,1,0:T(8,128)(2,1)S(1)} custom-call(s32[1]{0:T(128)} %bitcast.me.virt, bf16[8,768]{1,0:T(8,128)(2,1)} %refs_0_.1, bf16[8,256]{1,0:T(8,128)(2,1)} %refs_1_.1, bf16[2,8]{1,0:T(2,128)(2,1)} %refs_2_.1, bf16[3,8]{1,0:T(4,128)(2,1)} %refs_3_.1, bf16[32,256]{1,0:T(8,128)(2,1)} %refs_4_.1, bf16[32,256]{1,0:T(8,128)(2,1)} %bitcast.55), custom_call_target="tpu_custom_call" | custom-call | bytes 49236 | tf_op jit(solution)/shard_map/pack/pallas_call | solution.py:564
  1.6 5.1 %collective-permute-start.2 = (bf16[1,104,256]{2,1,0:T(8,128)(2,1)S(1)}, bf16[1,104,256]{2,1,0:T(8,128)(2,1)S(1)}, u32[]{:S(2)}, u32[]{:S(2)}) collective-permute-start(bf16[1,104,256]{2,1,0:T(8,128)(2,1)S(1)} %pack.1), channel_id=1, source_target_pairs={{0,24},{4,28},{8,16},{12,20},{16,8},{20,12},{24,0},{28,4},{1,25},{... | collective-permute-start | bytes 159752 | tf_op jit(solution)/shard_map/ppermute | solution.py:438
  6.7 0.0 collective-permute-start.1
  6.7 0.6 %collective-permute-start = (bf16[1,104,256]{2,1,0:T(8,128)(2,1)S(1)}, bf16[1,104,256]{2,1,0:T(8,128)(2,1)S(1)}, u32[]{:S(2)}, u32[]{:S(2)}) collective-permute-start(bf16[1,104,256]{2,1,0:T(8,128)(2,1)S(1)} %pack.1), channel_id=1, source_target_pairs={{0,8},{4,12},{8,0},{12,4},{16,24},{20,28},{24,16},{28,20},{1,9},{5... | collective-permute-start | bytes 159752 | tf_op jit(solution)/shard_map/ppermute | solution.py:438
  7.4 1.7 %turn.1 = (bf16[2304,256]{1,0:T(8,128)(2,1)S(1)}, bf16[256,2304]{1,0:T(8,128)(2,1)S(1)}, bf16[2304,256]{1,0:T(8,128)(2,1)S(1)}) custom-call(s32[1]{0:T(128)} %bitcast.me.virt, bf16[4608,256]{1,0:T(8,128)(2,1)} %bitcast.50, bf16[4608,256]{1,0:T(8,128)(2,1)} %bitcast.51), custom_call_target="tpu_custom_call" | custom-call | bytes 4718596 | tf_op jit(solution)/shard_map/turn/pallas_call | solution.py:564
  9.0 1.8 %collective-permute-done = bf16[1,104,256]{2,1,0:T(8,128)(2,1)S(1)} collective-permute-done((bf16[1,104,256]{2,1,0:T(8,128)(2,1)S(1)}, bf16[1,104,256]{2,1,0:T(8,128)(2,1)S(1)}, u32[]{:S(2)}, u32[]{:S(2)}) %collective-permute-start) | collective-permute-done | bytes 53280 | tf_op jit(solution)/shard_map/ppermute | solution.py:438
  10.9 0.0 collective-permute-done.2
  10.9 0.9 %collective-permute-done.1 = bf16[1,104,256]{2,1,0:T(8,128)(2,1)S(1)} collective-permute-done((bf16[1,104,256]{2,1,0:T(8,128)(2,1)S(1)}, bf16[1,104,256]{2,1,0:T(8,128)(2,1)S(1)}, u32[]{:S(2)}, u32[]{:S(2)}) %collective-permute-start.1) | collective-permute-done | bytes 53280 | tf_op jit(solution)/shard_map/ppermute | solution.py:438
  11.8 0.0 copy-start
  11.8 0.0 copy-start.1
  11.8 1.6 %collective-permute-start.3 = (bf16[136,256]{1,0:T(8,128)(2,1)S(1)}, bf16[136,256]{1,0:T(8,128)(2,1)S(1)}, u32[]{:S(2)}, u32[]{:S(2)}) collective-permute-start(bf16[136,256]{1,0:T(8,128)(2,1)S(1)} %get-tuple-element.116), channel_id=1, source_target_pairs={{0,4},{4,0},{8,12},{12,8},{16,20},{20,16},{24,28},{28,24},{1,5},{5... | collective-permute-start | bytes 208904 | tf_op jit(solution)/shard_map/ppermute | solution.py:438
  13.4 0.6 %collective-permute-start.6 = (bf16[4,64,256]{2,1,0:T(8,128)(2,1)S(1)}, bf16[4,64,256]{2,1,0:T(8,128)(2,1)S(1)}, u32[]{:S(2)}, u32[]{:S(2)}) collective-permute-start(bf16[4,64,256]{2,1,0:T(8,128)(2,1)S(1)} %pad_maximum_fusion), channel_id=1, source_target_pairs={{0,4},{4,0},{8,12},{12,8},{16,20},{20,16},{24,28},{28,24},{1,5},{5... | collective-permute-start | bytes 393224 | tf_op jit(solution)/shard_map/ppermute | solution.py:438
  14.0 1.5 %collective-permute-start.4 = (bf16[4,64,256]{2,1,0:T(8,128)(2,1)S(1)}, bf16[4,64,256]{2,1,0:T(8,128)(2,1)S(1)}, u32[]{:S(2)}, u32[]{:S(2)}) collective-permute-start(bf16[4,64,256]{2,1,0:T(8,128)(2,1)S(1)} %pad_maximum_fusion), channel_id=1, source_target_pairs={{0,2},{1,3},{2,0},{3,1},{4,6},{5,7},{6,4},{7,5},{8,10},{9,11},{10,... | collective-permute-start | bytes 393224 | tf_op jit(solution)/shard_map/ppermute | solution.py:438
  15.5 1.4 %collective-permute-done.3 = bf16[136,256]{1,0:T(8,128)(2,1)S(1)} collective-permute-done((bf16[136,256]{1,0:T(8,128)(2,1)S(1)}, bf16[136,256]{1,0:T(8,128)(2,1)S(1)}, u32[]{:S(2)}, u32[]{:S(2)}) %collective-permute-start.3) | collective-permute-done | bytes 69664 | tf_op jit(solution)/shard_map/ppermute | solution.py:438
  16.9 1.6 %collective-permute-start.5 = (bf16[264,256]{1,0:T(8,128)(2,1)S(1)}, bf16[264,256]{1,0:T(8,128)(2,1)S(1)}, u32[]{:S(2)}, u32[]{:S(2)}) collective-permute-start(bf16[264,256]{1,0:T(8,128)(2,1)S(1)} %constant_dynamic-update-slice_fusion.5), channel_id=1, source_target_pairs={{0,2},{1,3},{2,0},{3,1},{4,6},{5,7},{6,4},{7,5},{8,10},{9,11},{10,... | collective-permute-start | bytes 405512 | tf_op jit(solution)/shard_map/ppermute | solution.py:438
  18.5 1.1 %collective-permute-done.4 = bf16[4,64,256]{2,1,0:T(8,128)(2,1)S(1)} collective-permute-done((bf16[4,64,256]{2,1,0:T(8,128)(2,1)S(1)}, bf16[4,64,256]{2,1,0:T(8,128)(2,1)S(1)}, u32[]{:S(2)}, u32[]{:S(2)}) %collective-permute-start.4) | collective-permute-done | bytes 131104 | tf_op jit(solution)/shard_map/ppermute | solution.py:438
  19.6 1.0 %first_norm.1 = (f32[2304,256]{1,0:T(8,128)S(1)}, f32[2304,1]{1,0:T(8,128)S(1)}, bf16[272,2304]{1,0:T(8,128)(2,1)S(1)}) custom-call(bf16[2304,256]{1,0:T(8,128)(2,1)S(1)} %get-tuple-element.64.x_ref), custom_call_target="tpu_custom_call" | custom-call | bytes 1179648 | tf_op jit(solution)/shard_map/first_norm/pallas_call | solution.py:564
  20.6 0.0 collective-permute-done.6
  20.6 1.4 %collective-permute-done.5 = bf16[264,256]{1,0:T(8,128)(2,1)S(1)} collective-permute-done((bf16[264,256]{1,0:T(8,128)(2,1)S(1)}, bf16[264,256]{1,0:T(8,128)(2,1)S(1)}, u32[]{:S(2)}, u32[]{:S(2)}) %collective-permute-start.5) | collective-permute-done | bytes 135200 | tf_op jit(solution)/shard_map/ppermute | solution.py:438
  22.0 0.1 collective-permute-start.7
  22.1 0.5 collective-permute-start.10
  22.6 1.0 %collective-permute-start.8 = (bf16[4,64,256]{2,1,0:T(8,128)(2,1)S(1)}, bf16[4,64,256]{2,1,0:T(8,128)(2,1)S(1)}, u32[]{:S(2)}, u32[]{:S(2)}) collective-permute-start(bf16[4,64,256]{2,1,0:T(8,128)(2,1)S(1)} %collective-permute-done.4), channel_id=1, source_target_pairs={{0,4},{4,0},{8,12},{12,8},{16,20},{20,16},{24,28},{28,24},{1,5},{5... | collective-permute-start | bytes 393224 | tf_op jit(solution)/shard_map/ppermute | solution.py:438
  23.6 0.1 collective-permute-done.7.got
  23.7 0.0 copy-done
  23.7 0.0 copy-done.1
  23.7 3.6 %attend.1 = (bf16[2304,768]{1,0:T(8,128)(2,1)S(1)}, bf16[24,96,256]{2,1,0:T(8,128)(2,1)S(1)}, bf16[2304,256]{1,0:T(8,128)(2,1)S(1)}, f32[2304,256]{1,0:T(8,128)S...) custom-call(s32[1]{0:T(128)} %bitcast.me.virt, s32[1]{0:T(128)} %bitcast.me.virt, ...), custom_call_target="tpu_custom_call" | custom-call | flops 1434451968 | bytes 4071640 | tf_op jit(solution)/shard_map/attend/pallas_call | solution.py:564
  27.3 0.8 %collective-permute-done.8 = bf16[4,64,256]{2,1,0:T(8,128)(2,1)S(1)} collective-permute-done((bf16[4,64,256]{2,1,0:T(8,128)(2,1)S(1)}, bf16[4,64,256]{2,1,0:T(8,128)(2,1)S(1)}, u32[]{:S(2)}, u32[]{:S(2)}) %collective-permute-start.8) | collective-permute-done | bytes 131104 | tf_op jit(solution)/shard_map/ppermute | solution.py:438
  28.1 0.1 collective-permute-start.9
  28.2 0.0 collective-permute-done.10.got
  28.2 4.9 %hidden_near.1 = (bf16[2304,256]{1,0:T(8,128)(2,1)S(1)}, f32[2304,256]{1,0:T(8,128)S(1)}, f32[2304,1]{1,0:T(8,128)S(1)}, f32[2304,256]{1,0:T(8,128)S(1)}, f32[23...) custom-call(s32[1]{0:T(128)} %bitcast.me.virt, ...), custom_call_target="tpu_custom_call" | custom-call | flops 3623878656 | bytes 5251076 | tf_op jit(solution)/shard_map/hidden_near/pallas_call | solution.py:564
  33.1 0.6 collective-permute-start.12
  33.6 0.0 collective-permute-done.9.got
  33.6 4.5 %hidden_far.1 = (bf16[2304,256]{1,0:T(8,128)(2,1)S(1)}, f32[2304,256]{1,0:T(8,128)S(1)}, bf16[2304,256]{1,0:T(8,128)(2,1)S(1)}, f32[256,256]{1,0:T(8,128)S(1)}, f32[8,256]{1,0:T(8,128)S(1)}) custom-call(s32[1]{0:T(128)} %bitcast.me.virt, bf16[2304,256]{1,0:T(8,128)(2,1)S(1)} %get-tuple-element.62.cot_ref, f32[8,256]{1,0:T(8,128)S(1)} %get-tuple-element.93.vec, ...), custom_call_target="tpu_custom_call" | custom-call | flops 2717908992 | bytes 11158532 | tf_op jit(solution)/shard_map/hidden_far/pallas_call | solution.py:564
  38.2 0.0 collective-permute-done.12
  38.2 0.1 convert_add_fusion
  38.3 0.1 collective-permute-start.14
  38.4 1.0 %collective-permute-start.13 = (bf16[4,64,256]{2,1,0:T(8,128)(2,1)S(1)}, bf16[4,64,256]{2,1,0:T(8,128)(2,1)S(1)}, u32[]{:S(2)}, u32[]{:S(2)}) collective-permute-start(bf16[4,64,256]{2,1,0:T(8,128)(2,1)S(1)} %slice.253), channel_id=1, source_target_pairs={{0,4},{4,0},{8,12},{12,8},{16,20},{20,16},{24,28},{28,24},{1,5},{5... | collective-permute-start | bytes 393224 | tf_op jit(solution)/shard_map/ppermute | solution.py:438
  39.4 4.0 %back.1 = (bf16[2304,768]{1,0:T(8,128)(2,1)S(1)}, f32[8,32,256]{2,1,0:T(8,128)S(1)}, bf16[264,256]{1,0:T(8,128)(2,1)S(1)}, f32[8,256]{1,0:T(8,128)S(1)}) custom-call(s32[1]{0:T(128)} %bitcast.me.virt, bf16[2304,768]{1,0:T(8,128)(2,1)S(1)} %get-tuple-element.67.qkv_ref, bf16[24,96,256]{2,1,0:T(8,128)(2,1)S(1)} %get-tuple-element.68.prob_ref, ...), custom_call_target="tpu_custom_call" | custom-call | flops 1774190592 | bytes 7954436 | tf_op jit(solution)/shard_map/back/pallas_call | solution.py:564
  43.4 0.3 collective-permute-start.11
  43.6 0.7 %collective-permute-done.13 = bf16[4,64,256]{2,1,0:T(8,128)(2,1)S(1)} collective-permute-done((bf16[4,64,256]{2,1,0:T(8,128)(2,1)S(1)}, bf16[4,64,256]{2,1,0:T(8,128)(2,1)S(1)}, u32[]{:S(2)}, u32[]{:S(2)}) %collective-permute-start.13) | collective-permute-done | bytes 131104 | tf_op jit(solution)/shard_map/ppermute | solution.py:438
  44.4 0.8 %collective-permute-start.16 = (bf16[2,64,256]{2,1,0:T(8,128)(2,1)S(1)}, bf16[2,64,256]{2,1,0:T(8,128)(2,1)S(1)}, u32[]{:S(2)}, u32[]{:S(2)}) collective-permute-start(bf16[2,64,256]{2,1,0:T(8,128)(2,1)S(1)} %slice.254), channel_id=1, source_target_pairs={{0,8},{4,12},{8,0},{12,4},{16,24},{20,28},{24,16},{28,20},{1,9},{5... | collective-permute-start | bytes 196616 | tf_op jit(solution)/shard_map/ppermute | solution.py:438
  45.2 0.0 collective-permute-done.11
  45.3 1.0 %collective-permute-start.15 = (bf16[136,256]{1,0:T(8,128)(2,1)S(1)}, bf16[136,256]{1,0:T(8,128)(2,1)S(1)}, u32[]{:S(2)}, u32[]{:S(2)}) collective-permute-start(bf16[136,256]{1,0:T(8,128)(2,1)S(1)} %pad_maximum_fusion.1), channel_id=1, source_target_pairs={{0,4},{4,0},{8,12},{12,8},{16,20},{20,16},{24,28},{28,24},{1,5},{5... | collective-permute-start | bytes 208904 | tf_op jit(solution)/shard_map/ppermute | solution.py:438
  46.3 0.0 collective-permute-done.14.y_near
  46.3 1.8 %token_grad.1 = (f32[2304,256]{1,0:T(8,128)S(1)}, bf16[2304,256]{1,0:T(8,128)(2,1)S(1)}, bf16[4608,256]{1,0:T(8,128)(2,1)}) custom-call(s32[1]{0:T(128)} %bitcast.me.virt, bf16[2304,768]{1,0:T(8,128)(2,1)S(1)} %get-tuple-element.86.dqkv, bf16[256,768]{1,0:T(8,128)(2,1)S(1)} %get-tuple-element.82.wqkv, f32[8,256]{1,0:T(8,128)S(1)} %get-tuple-element.93.vec, ...), custom_call_target="tpu_custom_call" | custom-call | flops 905969664 | bytes 11027460 | tf_op jit(solution)/shard_map/token_grad/pallas_call | solution.py:564
  48.1 0.6 collective-permute-done.16
  48.7 1.0 %collective-permute-done.15 = bf16[136,256]{1,0:T(8,128)(2,1)S(1)} collective-permute-done((bf16[136,256]{1,0:T(8,128)(2,1)S(1)}, bf16[136,256]{1,0:T(8,128)(2,1)S(1)}, u32[]{:S(2)}, u32[]{:S(2)}) %collective-permute-start.15) | collective-permute-done | bytes 69664 | tf_op jit(solution)/shard_map/ppermute | solution.py:438
  49.7 0.1 collective-permute-start.17
  49.9 1.9 %collective-permute-start.19 = (bf16[104,256]{1,0:T(8,128)(2,1)S(1)}, bf16[104,256]{1,0:T(8,128)(2,1)S(1)}, u32[]{:S(2)}, u32[]{:S(2)}) collective-permute-start(bf16[104,256]{1,0:T(8,128)(2,1)S(1)} %pad_maximum_fusion.2), channel_id=1, source_target_pairs={{0,16},{4,20},{8,24},{12,28},{16,0},{20,4},{24,8},{28,12},{1,17},{... | collective-permute-start | bytes 159752 | tf_op jit(solution)/shard_map/ppermute | solution.py:438
  51.8 1.8 %collective-permute-start.20 = (bf16[40,256]{1,0:T(8,128)(2,1)S(1)}, bf16[40,256]{1,0:T(8,128)(2,1)S(1)}, u32[]{:S(2)}, u32[]{:S(2)}) collective-permute-start(bf16[40,256]{1,0:T(8,128)(2,1)S(1)} %get-tuple-element.143), channel_id=1, source_target_pairs={{0,24},{4,28},{8,16},{12,20},{16,8},{20,12},{24,0},{28,4},{1,25},{... | collective-permute-start | bytes 61448 | tf_op jit(solution)/shard_map/ppermute | solution.py:438
  53.6 0.0 collective-permute-start.18
  53.6 0.0 collective-permute-done.17.theirs
  53.6 2.2 %place.1 = f32[4608,256]{1,0:T(8,128)} custom-call(s32[1]{0:T(128)} %bitcast.me.virt, f32[2304,256]{1,0:T(8,128)S(1)} %get-tuple-element.99.mine, bf16[2304,256]{1,0:T(8,128)(2,1)S(1)} %collective-permute-done.17.theirs), custom_call_target="tpu_custom_call" | custom-call | bytes 3538948 | tf_op jit(solution)/shard_map/place/pallas_call | solution.py:564
  55.9 1.6 %collective-permute-done.20.refs_2_ = bf16[40,256]{1,0:T(8,128)(2,1)S(1)} collective-permute-done((bf16[40,256]{1,0:T(8,128)(2,1)S(1)}, bf16[40,256]{1,0:T(8,128)(2,1)S(1)}, u32[]{:S(2)}, u32[]{:S(2)}) %collective-permute-start.20) | collective-permute-done | bytes 20512 | tf_op jit(solution)/shard_map/ppermute | solution.py:438
  57.4 0.2 collective-permute-done.18.refs_0_
  57.6 0.0 collective-permute-done.19.refs_1_
  57.6 0.7 %finish.1 = (f32[8,768]{1,0:T(8,128)}, f32[8,256]{1,0:T(8,128)}, f32[2,8]{1,0:T(2,128)}, f32[3,8]{1,0:T(4,128)}, f32[32,256]{1,0:T(8,128)}, /*index=5*/f32[32,256]{1,0:T(8,128)}) custom-call(s32[1]{0:T(128)} %bitcast.me.virt, f32[4,32,256]{2,1,0:T(8,128)S(1)} %get-tuple-element.113.keep_a, f32[2,64,256]{2,1,0:T(8,128)S(1)} %slice_add_fusion.1.keep_b, ...), custom_call_target="tpu_custom_call" | custom-call | bytes 364548 | tf_op jit(solution)/shard_map/finish/pallas_call | solution.py:564
  (35 shorter events, 0.4 us)
Async XLA Ops:
  1.6 9.3 %collective-permute-start.2 = (bf16[1,104,256]{2,1,0:T(8,128)(2,1)S(1)}, bf16[1,104,256]{2,1,0:T(8,128)(2,1)S(1)}, u32[]{:S(2)}, u32[]{:S(2)}) collective-permute-start(bf16[1,104,256]{2,1,0:T(8,128)(2,1)S(1)} %pack.1), channel_id=1, source_target_pairs={{0,24},{4,28},{8,16},{12,20},{16,8},{20,12},{24,0},{28,4},{1,25},{... | collective-permute-start | bytes 159752 | tf_op jit(solution)/shard_map/ppermute | solution.py:438
  6.7 5.0 %collective-permute-start.1 = (bf16[1,104,256]{2,1,0:T(8,128)(2,1)S(1)}, bf16[1,104,256]{2,1,0:T(8,128)(2,1)S(1)}, u32[]{:S(2)}, u32[]{:S(2)}) collective-permute-start(bf16[1,104,256]{2,1,0:T(8,128)(2,1)S(1)} %pack.1), channel_id=1, source_target_pairs={{0,16},{4,20},{8,24},{12,28},{16,0},{20,4},{24,8},{28,12},{1,17},{... | collective-permute-start | bytes 159752 | tf_op jit(solution)/shard_map/ppermute | solution.py:438
  6.7 4.1 %collective-permute-start = (bf16[1,104,256]{2,1,0:T(8,128)(2,1)S(1)}, bf16[1,104,256]{2,1,0:T(8,128)(2,1)S(1)}, u32[]{:S(2)}, u32[]{:S(2)}) collective-permute-start(bf16[1,104,256]{2,1,0:T(8,128)(2,1)S(1)} %pack.1), channel_id=1, source_target_pairs={{0,8},{4,12},{8,0},{12,4},{16,24},{20,28},{24,16},{28,20},{1,9},{5... | collective-permute-start | bytes 159752 | tf_op jit(solution)/shard_map/ppermute | solution.py:438
  11.8 11.9 %copy-start = (s32[4,12]{1,0:T(4,128)S(1)}, s32[4,12]{1,0:T(4,128)}, u32[]{:S(2)}) copy-start(s32[4,12]{1,0:T(4,128)} %live.1) | copy-start | bytes 580
  11.8 11.8 %copy-start.1 = (s32[4]{0:T(128)S(1)}, s32[4]{0:T(128)}, u32[]{:S(2)}) copy-start(s32[4]{0:T(128)} %lens.1) | copy-start | bytes 52
  11.8 5.1 %collective-permute-start.3 = (bf16[136,256]{1,0:T(8,128)(2,1)S(1)}, bf16[136,256]{1,0:T(8,128)(2,1)S(1)}, u32[]{:S(2)}, u32[]{:S(2)}) collective-permute-start(bf16[136,256]{1,0:T(8,128)(2,1)S(1)} %get-tuple-element.116), channel_id=1, source_target_pairs={{0,4},{4,0},{8,12},{12,8},{16,20},{20,16},{24,28},{28,24},{1,5},{5... | collective-permute-start | bytes 208904 | tf_op jit(solution)/shard_map/ppermute | solution.py:438
  13.4 7.2 %collective-permute-start.6 = (bf16[4,64,256]{2,1,0:T(8,128)(2,1)S(1)}, bf16[4,64,256]{2,1,0:T(8,128)(2,1)S(1)}, u32[]{:S(2)}, u32[]{:S(2)}) collective-permute-start(bf16[4,64,256]{2,1,0:T(8,128)(2,1)S(1)} %pad_maximum_fusion), channel_id=1, source_target_pairs={{0,4},{4,0},{8,12},{12,8},{16,20},{20,16},{24,28},{28,24},{1,5},{5... | collective-permute-start | bytes 393224 | tf_op jit(solution)/shard_map/ppermute | solution.py:438
  14.0 5.6 %collective-permute-start.4 = (bf16[4,64,256]{2,1,0:T(8,128)(2,1)S(1)}, bf16[4,64,256]{2,1,0:T(8,128)(2,1)S(1)}, u32[]{:S(2)}, u32[]{:S(2)}) collective-permute-start(bf16[4,64,256]{2,1,0:T(8,128)(2,1)S(1)} %pad_maximum_fusion), channel_id=1, source_target_pairs={{0,2},{1,3},{2,0},{3,1},{4,6},{5,7},{6,4},{7,5},{8,10},{9,11},{10,... | collective-permute-start | bytes 393224 | tf_op jit(solution)/shard_map/ppermute | solution.py:438
  16.9 5.1 %collective-permute-start.5 = (bf16[264,256]{1,0:T(8,128)(2,1)S(1)}, bf16[264,256]{1,0:T(8,128)(2,1)S(1)}, u32[]{:S(2)}, u32[]{:S(2)}) collective-permute-start(bf16[264,256]{1,0:T(8,128)(2,1)S(1)} %constant_dynamic-update-slice_fusion.5), channel_id=1, source_target_pairs={{0,2},{1,3},{2,0},{3,1},{4,6},{5,7},{6,4},{7,5},{8,10},{9,11},{10,... | collective-permute-start | bytes 405512 | tf_op jit(solution)/shard_map/ppermute | solution.py:438
  22.0 1.6 %collective-permute-start.7 = (bf16[520,256]{1,0:T(8,128)(2,1)S(1)}, bf16[520,256]{1,0:T(8,128)(2,1)S(1)}, u32[]{:S(2)}, u32[]{:S(2)}) collective-permute-start(bf16[520,256]{1,0:T(8,128)(2,1)S(1)} %constant_dynamic-update-slice_fusion.15.held), channel_id=1, source_target_pairs={{0,1},{1,0},{2,3},{3,2},{4,5},{5,4},{6,7},{7,6},{8,9},{9,8},{10,11... | collective-permute-start | bytes 798728 | tf_op jit(solution)/shard_map/ppermute | solution.py:438
  22.1 6.1 %collective-permute-start.10 = (bf16[8,64,256]{2,1,0:T(8,128)(2,1)S(1)}, bf16[8,64,256]{2,1,0:T(8,128)(2,1)S(1)}, u32[]{:S(2)}, u32[]{:S(2)}) collective-permute-start(bf16[8,64,256]{2,1,0:T(8,128)(2,1)S(1)} %constant_dynamic-update-slice_fusion.10.own), channel_id=1, source_target_pairs={{0,1},{1,0},{2,3},{3,2},{4,5},{5,4},{6,7},{7,6},{8,9},{9,8},{10,11... | collective-permute-start | bytes 786440 | tf_op jit(solution)/shard_map/ppermute | solution.py:438
  22.6 5.5 %collective-permute-start.8 = (bf16[4,64,256]{2,1,0:T(8,128)(2,1)S(1)}, bf16[4,64,256]{2,1,0:T(8,128)(2,1)S(1)}, u32[]{:S(2)}, u32[]{:S(2)}) collective-permute-start(bf16[4,64,256]{2,1,0:T(8,128)(2,1)S(1)} %collective-permute-done.4), channel_id=1, source_target_pairs={{0,4},{4,0},{8,12},{12,8},{16,20},{20,16},{24,28},{28,24},{1,5},{5... | collective-permute-start | bytes 393224 | tf_op jit(solution)/shard_map/ppermute | solution.py:438
  28.1 5.5 %collective-permute-start.9 = (bf16[8,64,256]{2,1,0:T(8,128)(2,1)S(1)}, bf16[8,64,256]{2,1,0:T(8,128)(2,1)S(1)}, u32[]{:S(2)}, u32[]{:S(2)}) collective-permute-start(bf16[8,64,256]{2,1,0:T(8,128)(2,1)S(1)} %constant_dynamic-update-slice_fusion.20.own), channel_id=1, source_target_pairs={{0,1},{1,0},{2,3},{3,2},{4,5},{5,4},{6,7},{7,6},{8,9},{9,8},{10,11... | collective-permute-start | bytes 786440 | tf_op jit(solution)/shard_map/ppermute | solution.py:438
  33.1 5.1 %collective-permute-start.12 = (bf16[8,64,256]{2,1,0:T(8,128)(2,1)S(1)}, bf16[8,64,256]{2,1,0:T(8,128)(2,1)S(1)}, u32[]{:S(2)}, u32[]{:S(2)}) collective-permute-start(bf16[8,64,256]{2,1,0:T(8,128)(2,1)S(1)} %get-tuple-element.90), channel_id=1, source_target_pairs={{0,1},{1,0},{2,3},{3,2},{4,5},{5,4},{6,7},{7,6},{8,9},{9,8},{10,11... | collective-permute-start | bytes 786440 | tf_op jit(solution)/shard_map/ppermute | solution.py:438
  38.3 8.1 %collective-permute-start.14 = (bf16[2304,256]{1,0:T(8,128)(2,1)S(1)}, bf16[2304,256]{1,0:T(8,128)(2,1)S(1)}, u32[]{:S(2)}, u32[]{:S(2)}) collective-permute-start(bf16[2304,256]{1,0:T(8,128)(2,1)S(1)} %get-tuple-element.97.y), channel_id=1, source_target_pairs={{0,1},{1,0},{2,3},{3,2},{4,5},{5,4},{6,7},{7,6},{8,9},{9,8},{10,11... | collective-permute-start | bytes 3538952 | tf_op jit(solution)/shard_map/ppermute | solution.py:438
  38.4 5.9 %collective-permute-start.13 = (bf16[4,64,256]{2,1,0:T(8,128)(2,1)S(1)}, bf16[4,64,256]{2,1,0:T(8,128)(2,1)S(1)}, u32[]{:S(2)}, u32[]{:S(2)}) collective-permute-start(bf16[4,64,256]{2,1,0:T(8,128)(2,1)S(1)} %slice.253), channel_id=1, source_target_pairs={{0,4},{4,0},{8,12},{12,8},{16,20},{20,16},{24,28},{28,24},{1,5},{5... | collective-permute-start | bytes 393224 | tf_op jit(solution)/shard_map/ppermute | solution.py:438
  43.4 1.8 %collective-permute-start.11 = (bf16[264,256]{1,0:T(8,128)(2,1)S(1)}, bf16[264,256]{1,0:T(8,128)(2,1)S(1)}, u32[]{:S(2)}, u32[]{:S(2)}) collective-permute-start(bf16[264,256]{1,0:T(8,128)(2,1)S(1)} %get-tuple-element.88), channel_id=1, source_target_pairs={{0,1},{1,0},{2,3},{3,2},{4,5},{5,4},{6,7},{7,6},{8,9},{9,8},{10,11... | collective-permute-start | bytes 405512 | tf_op jit(solution)/shard_map/ppermute | solution.py:438
  44.4 4.3 %collective-permute-start.16 = (bf16[2,64,256]{2,1,0:T(8,128)(2,1)S(1)}, bf16[2,64,256]{2,1,0:T(8,128)(2,1)S(1)}, u32[]{:S(2)}, u32[]{:S(2)}) collective-permute-start(bf16[2,64,256]{2,1,0:T(8,128)(2,1)S(1)} %slice.254), channel_id=1, source_target_pairs={{0,8},{4,12},{8,0},{12,4},{16,24},{20,28},{24,16},{28,20},{1,9},{5... | collective-permute-start | bytes 196616 | tf_op jit(solution)/shard_map/ppermute | solution.py:438
  45.3 4.4 %collective-permute-start.15 = (bf16[136,256]{1,0:T(8,128)(2,1)S(1)}, bf16[136,256]{1,0:T(8,128)(2,1)S(1)}, u32[]{:S(2)}, u32[]{:S(2)}) collective-permute-start(bf16[136,256]{1,0:T(8,128)(2,1)S(1)} %pad_maximum_fusion.1), channel_id=1, source_target_pairs={{0,4},{4,0},{8,12},{12,8},{16,20},{20,16},{24,28},{28,24},{1,5},{5... | collective-permute-start | bytes 208904 | tf_op jit(solution)/shard_map/ppermute | solution.py:438
  49.7 3.9 %collective-permute-start.17 = (bf16[2304,256]{1,0:T(8,128)(2,1)S(1)}, bf16[2304,256]{1,0:T(8,128)(2,1)S(1)}, u32[]{:S(2)}, u32[]{:S(2)}) collective-permute-start(bf16[2304,256]{1,0:T(8,128)(2,1)S(1)} %get-tuple-element.104), channel_id=1, source_target_pairs={{0,1},{1,0},{2,3},{3,2},{4,5},{5,4},{6,7},{7,6},{8,9},{9,8},{10,11... | collective-permute-start | bytes 3538952 | tf_op jit(solution)/shard_map/ppermute | solution.py:438
  49.9 7.7 %collective-permute-start.19 = (bf16[104,256]{1,0:T(8,128)(2,1)S(1)}, bf16[104,256]{1,0:T(8,128)(2,1)S(1)}, u32[]{:S(2)}, u32[]{:S(2)}) collective-permute-start(bf16[104,256]{1,0:T(8,128)(2,1)S(1)} %pad_maximum_fusion.2), channel_id=1, source_target_pairs={{0,16},{4,20},{8,24},{12,28},{16,0},{20,4},{24,8},{28,12},{1,17},{... | collective-permute-start | bytes 159752 | tf_op jit(solution)/shard_map/ppermute | solution.py:438
  51.8 5.6 %collective-permute-start.20 = (bf16[40,256]{1,0:T(8,128)(2,1)S(1)}, bf16[40,256]{1,0:T(8,128)(2,1)S(1)}, u32[]{:S(2)}, u32[]{:S(2)}) collective-permute-start(bf16[40,256]{1,0:T(8,128)(2,1)S(1)} %get-tuple-element.143), channel_id=1, source_target_pairs={{0,24},{4,28},{8,16},{12,20},{16,8},{20,12},{24,0},{28,4},{1,25},{... | collective-permute-start | bytes 61448 | tf_op jit(solution)/shard_map/ppermute | solution.py:438
  53.6 4.0 %collective-permute-start.18 = (bf16[40,256]{1,0:T(8,128)(2,1)S(1)}, bf16[40,256]{1,0:T(8,128)(2,1)S(1)}, u32[]{:S(2)}, u32[]{:S(2)}) collective-permute-start(bf16[40,256]{1,0:T(8,128)(2,1)S(1)} %get-tuple-element.144), channel_id=1, source_target_pairs={{0,8},{4,12},{8,0},{12,4},{16,24},{20,28},{24,16},{28,20},{1,9},{5... | collective-permute-start | bytes 61448 | tf_op jit(solution)/shard_map/ppermute | solution.py:438

commit v2 on v1

--- a/solution.py
+++ b/solution.py
@@ -673,7 +673,7 @@
         far_b = jnp.concatenate([far_b, after(far_x, x1)], 0)
         got_far = swap(far_b, "tensor", 1)
         got_b = after(got_b, far_b)
-    wide_per = 8 if rows % 8 == 0 else rows
+    wide_per = 4 if rows % 4 == 0 else rows
     *first, keep_b, send_b = call(
         functools.partial(hidden_near_kernel, wide_per),
         "hidden_near",

time: 58.6 us -> 59.1 us (level)
  no operation moved by 1% of the time
where the time goes in v2:
time: 59.1 us; the launch traced here: 58.8 us
  Pallas kernels  25.7 us (43%)
  starting transfers between devices  20.2 us (34%)
  waiting for transfers between devices  11.4 us (19%)
  between operations  0.97 us (2%)
    pallas_call x10, Pallas kernels, call(): pl.pallas_call(kernel, name=name, out_shape=outs, in_specs=[pl.BlockSpec(...  25.7 us
    ppermute x21, starting transfers between devices, swap(): return lax.ppermute(block, axis, [(i, i ^ bit) for i in range(size)])  20.2 us
    ppermute x21, waiting for transfers between devices, swap(): return lax.ppermute(block, axis, [(i, i ^ bit) for i in range(size)])  11.4 us
  transfers between devices with their start and end apart: 21, of which 12 were waited for; matrix products, arithmetic and copies ran while one was open for 1% of the time, Pallas kernels for 41%

profile of v2, /device:TPU:0, one launch (start us, length us, event | category | flops | bytes accessed | tf_op | source)
XLA Modules:
  0.0 58.8 jit_solution(15620184174024684467)
XLA Ops:
  0.6 0.9 %pack.1 = bf16[1,104,256]{2,1,0:T(8,128)(2,1)S(1)} custom-call(s32[1]{0:T(128)} %bitcast.me.virt, bf16[8,768]{1,0:T(8,128)(2,1)} %refs_0_.1, bf16[8,256]{1,0:T(8,128)(2,1)} %refs_1_.1, bf16[2,8]{1,0:T(2,128)(2,1)} %refs_2_.1, bf16[3,8]{1,0:T(4,128)(2,1)} %refs_3_.1, bf16[32,256]{1,0:T(8,128)(2,1)} %refs_4_.1, bf16[32,256]{1,0:T(8,128)(2,1)} %bitcast.55), custom_call_target="tpu_custom_call" | custom-call | bytes 49236 | tf_op jit(solution)/shard_map/pack/pallas_call | solution.py:564
  1.6 5.1 %collective-permute-start.2 = (bf16[1,104,256]{2,1,0:T(8,128)(2,1)S(1)}, bf16[1,104,256]{2,1,0:T(8,128)(2,1)S(1)}, u32[]{:S(2)}, u32[]{:S(2)}) collective-permute-start(bf16[1,104,256]{2,1,0:T(8,128)(2,1)S(1)} %pack.1), channel_id=1, source_target_pairs={{0,24},{4,28},{8,16},{12,20},{16,8},{20,12},{24,0},{28,4},{1,25},{... | collective-permute-start | bytes 159752 | tf_op jit(solution)/shard_map/ppermute | solution.py:438
  6.7 0.0 collective-permute-start.1
  6.7 0.6 %collective-permute-start = (bf16[1,104,256]{2,1,0:T(8,128)(2,1)S(1)}, bf16[1,104,256]{2,1,0:T(8,128)(2,1)S(1)}, u32[]{:S(2)}, u32[]{:S(2)}) collective-permute-start(bf16[1,104,256]{2,1,0:T(8,128)(2,1)S(1)} %pack.1), channel_id=1, source_target_pairs={{0,8},{4,12},{8,0},{12,4},{16,24},{20,28},{24,16},{28,20},{1,9},{5... | collective-permute-start | bytes 159752 | tf_op jit(solution)/shard_map/ppermute | solution.py:438
  7.4 1.7 %turn.1 = (bf16[2304,256]{1,0:T(8,128)(2,1)S(1)}, bf16[256,2304]{1,0:T(8,128)(2,1)S(1)}, bf16[2304,256]{1,0:T(8,128)(2,1)S(1)}) custom-call(s32[1]{0:T(128)} %bitcast.me.virt, bf16[4608,256]{1,0:T(8,128)(2,1)} %bitcast.50, bf16[4608,256]{1,0:T(8,128)(2,1)} %bitcast.51), custom_call_target="tpu_custom_call" | custom-call | bytes 4718596 | tf_op jit(solution)/shard_map/turn/pallas_call | solution.py:564
  9.0 1.8 %collective-permute-done = bf16[1,104,256]{2,1,0:T(8,128)(2,1)S(1)} collective-permute-done((bf16[1,104,256]{2,1,0:T(8,128)(2,1)S(1)}, bf16[1,104,256]{2,1,0:T(8,128)(2,1)S(1)}, u32[]{:S(2)}, u32[]{:S(2)}) %collective-permute-start) | collective-permute-done | bytes 53280 | tf_op jit(solution)/shard_map/ppermute | solution.py:438
  10.9 0.0 collective-permute-done.2
  10.9 0.9 %collective-permute-done.1 = bf16[1,104,256]{2,1,0:T(8,128)(2,1)S(1)} collective-permute-done((bf16[1,104,256]{2,1,0:T(8,128)(2,1)S(1)}, bf16[1,104,256]{2,1,0:T(8,128)(2,1)S(1)}, u32[]{:S(2)}, u32[]{:S(2)}) %collective-permute-start.1) | collective-permute-done | bytes 53280 | tf_op jit(solution)/shard_map/ppermute | solution.py:438
  11.8 0.0 copy-start
  11.8 0.0 copy-start.1
  11.8 1.6 %collective-permute-start.3 = (bf16[136,256]{1,0:T(8,128)(2,1)S(1)}, bf16[136,256]{1,0:T(8,128)(2,1)S(1)}, u32[]{:S(2)}, u32[]{:S(2)}) collective-permute-start(bf16[136,256]{1,0:T(8,128)(2,1)S(1)} %get-tuple-element.116), channel_id=1, source_target_pairs={{0,4},{4,0},{8,12},{12,8},{16,20},{20,16},{24,28},{28,24},{1,5},{5... | collective-permute-start | bytes 208904 | tf_op jit(solution)/shard_map/ppermute | solution.py:438
  13.4 0.6 %collective-permute-start.6 = (bf16[4,64,256]{2,1,0:T(8,128)(2,1)S(1)}, bf16[4,64,256]{2,1,0:T(8,128)(2,1)S(1)}, u32[]{:S(2)}, u32[]{:S(2)}) collective-permute-start(bf16[4,64,256]{2,1,0:T(8,128)(2,1)S(1)} %pad_maximum_fusion), channel_id=1, source_target_pairs={{0,4},{4,0},{8,12},{12,8},{16,20},{20,16},{24,28},{28,24},{1,5},{5... | collective-permute-start | bytes 393224 | tf_op jit(solution)/shard_map/ppermute | solution.py:438
  14.0 1.5 %collective-permute-start.4 = (bf16[4,64,256]{2,1,0:T(8,128)(2,1)S(1)}, bf16[4,64,256]{2,1,0:T(8,128)(2,1)S(1)}, u32[]{:S(2)}, u32[]{:S(2)}) collective-permute-start(bf16[4,64,256]{2,1,0:T(8,128)(2,1)S(1)} %pad_maximum_fusion), channel_id=1, source_target_pairs={{0,2},{1,3},{2,0},{3,1},{4,6},{5,7},{6,4},{7,5},{8,10},{9,11},{10,... | collective-permute-start | bytes 393224 | tf_op jit(solution)/shard_map/ppermute | solution.py:438
  15.5 1.4 %collective-permute-done.3 = bf16[136,256]{1,0:T(8,128)(2,1)S(1)} collective-permute-done((bf16[136,256]{1,0:T(8,128)(2,1)S(1)}, bf16[136,256]{1,0:T(8,128)(2,1)S(1)}, u32[]{:S(2)}, u32[]{:S(2)}) %collective-permute-start.3) | collective-permute-done | bytes 69664 | tf_op jit(solution)/shard_map/ppermute | solution.py:438
  16.9 1.6 %collective-permute-start.5 = (bf16[264,256]{1,0:T(8,128)(2,1)S(1)}, bf16[264,256]{1,0:T(8,128)(2,1)S(1)}, u32[]{:S(2)}, u32[]{:S(2)}) collective-permute-start(bf16[264,256]{1,0:T(8,128)(2,1)S(1)} %constant_dynamic-update-slice_fusion.5), channel_id=1, source_target_pairs={{0,2},{1,3},{2,0},{3,1},{4,6},{5,7},{6,4},{7,5},{8,10},{9,11},{10,... | collective-permute-start | bytes 405512 | tf_op jit(solution)/shard_map/ppermute | solution.py:438
  18.5 1.1 %collective-permute-done.4 = bf16[4,64,256]{2,1,0:T(8,128)(2,1)S(1)} collective-permute-done((bf16[4,64,256]{2,1,0:T(8,128)(2,1)S(1)}, bf16[4,64,256]{2,1,0:T(8,128)(2,1)S(1)}, u32[]{:S(2)}, u32[]{:S(2)}) %collective-permute-start.4) | collective-permute-done | bytes 131104 | tf_op jit(solution)/shard_map/ppermute | solution.py:438
  19.6 1.0 %first_norm.1 = (f32[2304,256]{1,0:T(8,128)S(1)}, f32[2304,1]{1,0:T(8,128)S(1)}, bf16[272,2304]{1,0:T(8,128)(2,1)S(1)}) custom-call(bf16[2304,256]{1,0:T(8,128)(2,1)S(1)} %get-tuple-element.64.x_ref), custom_call_target="tpu_custom_call" | custom-call | bytes 1179648 | tf_op jit(solution)/shard_map/first_norm/pallas_call | solution.py:564
  20.6 0.0 collective-permute-done.6
  20.6 1.4 %collective-permute-done.5 = bf16[264,256]{1,0:T(8,128)(2,1)S(1)} collective-permute-done((bf16[264,256]{1,0:T(8,128)(2,1)S(1)}, bf16[264,256]{1,0:T(8,128)(2,1)S(1)}, u32[]{:S(2)}, u32[]{:S(2)}) %collective-permute-start.5) | collective-permute-done | bytes 135200 | tf_op jit(solution)/shard_map/ppermute | solution.py:438
  22.0 0.1 collective-permute-start.7
  22.1 0.5 collective-permute-start.10
  22.6 1.0 %collective-permute-start.8 = (bf16[4,64,256]{2,1,0:T(8,128)(2,1)S(1)}, bf16[4,64,256]{2,1,0:T(8,128)(2,1)S(1)}, u32[]{:S(2)}, u32[]{:S(2)}) collective-permute-start(bf16[4,64,256]{2,1,0:T(8,128)(2,1)S(1)} %collective-permute-done.4), channel_id=1, source_target_pairs={{0,4},{4,0},{8,12},{12,8},{16,20},{20,16},{24,28},{28,24},{1,5},{5... | collective-permute-start | bytes 393224 | tf_op jit(solution)/shard_map/ppermute | solution.py:438
  23.6 0.1 collective-permute-done.7.got
  23.7 0.0 copy-done
  23.7 0.0 copy-done.1
  23.7 3.6 %attend.1 = (bf16[2304,768]{1,0:T(8,128)(2,1)S(1)}, bf16[24,96,256]{2,1,0:T(8,128)(2,1)S(1)}, bf16[2304,256]{1,0:T(8,128)(2,1)S(1)}, f32[2304,256]{1,0:T(8,128)S...) custom-call(s32[1]{0:T(128)} %bitcast.me.virt, s32[1]{0:T(128)} %bitcast.me.virt, ...), custom_call_target="tpu_custom_call" | custom-call | flops 1434451968 | bytes 4071640 | tf_op jit(solution)/shard_map/attend/pallas_call | solution.py:564
  27.3 0.8 %collective-permute-done.8 = bf16[4,64,256]{2,1,0:T(8,128)(2,1)S(1)} collective-permute-done((bf16[4,64,256]{2,1,0:T(8,128)(2,1)S(1)}, bf16[4,64,256]{2,1,0:T(8,128)(2,1)S(1)}, u32[]{:S(2)}, u32[]{:S(2)}) %collective-permute-start.8) | collective-permute-done | bytes 131104 | tf_op jit(solution)/shard_map/ppermute | solution.py:438
  28.1 0.1 collective-permute-start.9
  28.2 0.0 collective-permute-done.10.got
  28.2 4.9 %hidden_near.1 = (bf16[2304,256]{1,0:T(8,128)(2,1)S(1)}, f32[2304,256]{1,0:T(8,128)S(1)}, f32[2304,1]{1,0:T(8,128)S(1)}, f32[2304,256]{1,0:T(8,128)S(1)}, f32[23...) custom-call(s32[1]{0:T(128)} %bitcast.me.virt, ...), custom_call_target="tpu_custom_call" | custom-call | flops 3623878656 | bytes 5251076 | tf_op jit(solution)/shard_map/hidden_near/pallas_call | solution.py:564
  33.1 0.5 collective-permute-start.12
  33.6 0.0 collective-permute-done.9.got
  33.6 5.0 %hidden_far.1 = (bf16[2304,256]{1,0:T(8,128)(2,1)S(1)}, f32[2304,256]{1,0:T(8,128)S(1)}, bf16[2304,256]{1,0:T(8,128)(2,1)S(1)}, f32[256,256]{1,0:T(8,128)S(1)}, f32[8,256]{1,0:T(8,128)S(1)}) custom-call(s32[1]{0:T(128)} %bitcast.me.virt, bf16[2304,256]{1,0:T(8,128)(2,1)S(1)} %get-tuple-element.62.cot_ref, f32[8,256]{1,0:T(8,128)S(1)} %get-tuple-element.93.vec, ...), custom_call_target="tpu_custom_call" | custom-call | flops 2717908992 | bytes 11158532 | tf_op jit(solution)/shard_map/hidden_far/pallas_call | solution.py:564
  38.6 0.0 collective-permute-done.12
  38.7 0.1 convert_add_fusion
  38.7 0.1 collective-permute-start.14
  38.9 1.0 %collective-permute-start.13 = (bf16[4,64,256]{2,1,0:T(8,128)(2,1)S(1)}, bf16[4,64,256]{2,1,0:T(8,128)(2,1)S(1)}, u32[]{:S(2)}, u32[]{:S(2)}) collective-permute-start(bf16[4,64,256]{2,1,0:T(8,128)(2,1)S(1)} %slice.253), channel_id=1, source_target_pairs={{0,4},{4,0},{8,12},{12,8},{16,20},{20,16},{24,28},{28,24},{1,5},{5... | collective-permute-start | bytes 393224 | tf_op jit(solution)/shard_map/ppermute | solution.py:438
  39.9 4.0 %back.1 = (bf16[2304,768]{1,0:T(8,128)(2,1)S(1)}, f32[8,32,256]{2,1,0:T(8,128)S(1)}, bf16[264,256]{1,0:T(8,128)(2,1)S(1)}, f32[8,256]{1,0:T(8,128)S(1)}) custom-call(s32[1]{0:T(128)} %bitcast.me.virt, bf16[2304,768]{1,0:T(8,128)(2,1)S(1)} %get-tuple-element.67.qkv_ref, bf16[24,96,256]{2,1,0:T(8,128)(2,1)S(1)} %get-tuple-element.68.prob_ref, ...), custom_call_target="tpu_custom_call" | custom-call | flops 1774190592 | bytes 7954436 | tf_op jit(solution)/shard_map/back/pallas_call | solution.py:564
  43.9 0.3 collective-permute-start.11
  44.1 0.7 %collective-permute-done.13 = bf16[4,64,256]{2,1,0:T(8,128)(2,1)S(1)} collective-permute-done((bf16[4,64,256]{2,1,0:T(8,128)(2,1)S(1)}, bf16[4,64,256]{2,1,0:T(8,128)(2,1)S(1)}, u32[]{:S(2)}, u32[]{:S(2)}) %collective-permute-start.13) | collective-permute-done | bytes 131104 | tf_op jit(solution)/shard_map/ppermute | solution.py:438
  44.8 0.8 %collective-permute-start.16 = (bf16[2,64,256]{2,1,0:T(8,128)(2,1)S(1)}, bf16[2,64,256]{2,1,0:T(8,128)(2,1)S(1)}, u32[]{:S(2)}, u32[]{:S(2)}) collective-permute-start(bf16[2,64,256]{2,1,0:T(8,128)(2,1)S(1)} %slice.254), channel_id=1, source_target_pairs={{0,8},{4,12},{8,0},{12,4},{16,24},{20,28},{24,16},{28,20},{1,9},{5... | collective-permute-start | bytes 196616 | tf_op jit(solution)/shard_map/ppermute | solution.py:438
  45.7 0.0 collective-permute-done.11
  45.8 1.0 %collective-permute-start.15 = (bf16[136,256]{1,0:T(8,128)(2,1)S(1)}, bf16[136,256]{1,0:T(8,128)(2,1)S(1)}, u32[]{:S(2)}, u32[]{:S(2)}) collective-permute-start(bf16[136,256]{1,0:T(8,128)(2,1)S(1)} %pad_maximum_fusion.1), channel_id=1, source_target_pairs={{0,4},{4,0},{8,12},{12,8},{16,20},{20,16},{24,28},{28,24},{1,5},{5... | collective-permute-start | bytes 208904 | tf_op jit(solution)/shard_map/ppermute | solution.py:438
  46.8 0.0 collective-permute-done.14.y_near
  46.8 1.8 %token_grad.1 = (f32[2304,256]{1,0:T(8,128)S(1)}, bf16[2304,256]{1,0:T(8,128)(2,1)S(1)}, bf16[4608,256]{1,0:T(8,128)(2,1)}) custom-call(s32[1]{0:T(128)} %bitcast.me.virt, bf16[2304,768]{1,0:T(8,128)(2,1)S(1)} %get-tuple-element.86.dqkv, bf16[256,768]{1,0:T(8,128)(2,1)S(1)} %get-tuple-element.82.wqkv, f32[8,256]{1,0:T(8,128)S(1)} %get-tuple-element.93.vec, ...), custom_call_target="tpu_custom_call" | custom-call | flops 905969664 | bytes 11027460 | tf_op jit(solution)/shard_map/token_grad/pallas_call | solution.py:564
  48.6 0.6 collective-permute-done.16
  49.2 1.0 %collective-permute-done.15 = bf16[136,256]{1,0:T(8,128)(2,1)S(1)} collective-permute-done((bf16[136,256]{1,0:T(8,128)(2,1)S(1)}, bf16[136,256]{1,0:T(8,128)(2,1)S(1)}, u32[]{:S(2)}, u32[]{:S(2)}) %collective-permute-start.15) | collective-permute-done | bytes 69664 | tf_op jit(solution)/shard_map/ppermute | solution.py:438
  50.2 0.1 collective-permute-start.17
  50.4 1.9 %collective-permute-start.19 = (bf16[104,256]{1,0:T(8,128)(2,1)S(1)}, bf16[104,256]{1,0:T(8,128)(2,1)S(1)}, u32[]{:S(2)}, u32[]{:S(2)}) collective-permute-start(bf16[104,256]{1,0:T(8,128)(2,1)S(1)} %pad_maximum_fusion.2), channel_id=1, source_target_pairs={{0,16},{4,20},{8,24},{12,28},{16,0},{20,4},{24,8},{28,12},{1,17},{... | collective-permute-start | bytes 159752 | tf_op jit(solution)/shard_map/ppermute | solution.py:438
  52.3 1.8 %collective-permute-start.20 = (bf16[40,256]{1,0:T(8,128)(2,1)S(1)}, bf16[40,256]{1,0:T(8,128)(2,1)S(1)}, u32[]{:S(2)}, u32[]{:S(2)}) collective-permute-start(bf16[40,256]{1,0:T(8,128)(2,1)S(1)} %get-tuple-element.143), channel_id=1, source_target_pairs={{0,24},{4,28},{8,16},{12,20},{16,8},{20,12},{24,0},{28,4},{1,25},{... | collective-permute-start | bytes 61448 | tf_op jit(solution)/shard_map/ppermute | solution.py:438
  54.1 0.0 collective-permute-start.18
  54.1 0.0 collective-permute-done.17.theirs
  54.1 2.2 %place.1 = f32[4608,256]{1,0:T(8,128)} custom-call(s32[1]{0:T(128)} %bitcast.me.virt, f32[2304,256]{1,0:T(8,128)S(1)} %get-tuple-element.99.mine, bf16[2304,256]{1,0:T(8,128)(2,1)S(1)} %collective-permute-done.17.theirs), custom_call_target="tpu_custom_call" | custom-call | bytes 3538948 | tf_op jit(solution)/shard_map/place/pallas_call | solution.py:564
  56.3 1.6 %collective-permute-done.20.refs_2_ = bf16[40,256]{1,0:T(8,128)(2,1)S(1)} collective-permute-done((bf16[40,256]{1,0:T(8,128)(2,1)S(1)}, bf16[40,256]{1,0:T(8,128)(2,1)S(1)}, u32[]{:S(2)}, u32[]{:S(2)}) %collective-permute-start.20) | collective-permute-done | bytes 20512 | tf_op jit(solution)/shard_map/ppermute | solution.py:438
  57.9 0.2 collective-permute-done.18.refs_0_
  58.1 0.0 collective-permute-done.19.refs_1_
  58.1 0.7 %finish.1 = (f32[8,768]{1,0:T(8,128)}, f32[8,256]{1,0:T(8,128)}, f32[2,8]{1,0:T(2,128)}, f32[3,8]{1,0:T(4,128)}, f32[32,256]{1,0:T(8,128)}, /*index=5*/f32[32,256]{1,0:T(8,128)}) custom-call(s32[1]{0:T(128)} %bitcast.me.virt, f32[4,32,256]{2,1,0:T(8,128)S(1)} %get-tuple-element.113.keep_a, f32[2,64,256]{2,1,0:T(8,128)S(1)} %slice_add_fusion.1.keep_b, ...), custom_call_target="tpu_custom_call" | custom-call | bytes 364548 | tf_op jit(solution)/shard_map/finish/pallas_call | solution.py:564
  (35 shorter events, 0.4 us)
Async XLA Ops:
  1.6 9.3 %collective-permute-start.2 = (bf16[1,104,256]{2,1,0:T(8,128)(2,1)S(1)}, bf16[1,104,256]{2,1,0:T(8,128)(2,1)S(1)}, u32[]{:S(2)}, u32[]{:S(2)}) collective-permute-start(bf16[1,104,256]{2,1,0:T(8,128)(2,1)S(1)} %pack.1), channel_id=1, source_target_pairs={{0,24},{4,28},{8,16},{12,20},{16,8},{20,12},{24,0},{28,4},{1,25},{... | collective-permute-start | bytes 159752 | tf_op jit(solution)/shard_map/ppermute | solution.py:438
  6.7 5.0 %collective-permute-start.1 = (bf16[1,104,256]{2,1,0:T(8,128)(2,1)S(1)}, bf16[1,104,256]{2,1,0:T(8,128)(2,1)S(1)}, u32[]{:S(2)}, u32[]{:S(2)}) collective-permute-start(bf16[1,104,256]{2,1,0:T(8,128)(2,1)S(1)} %pack.1), channel_id=1, source_target_pairs={{0,16},{4,20},{8,24},{12,28},{16,0},{20,4},{24,8},{28,12},{1,17},{... | collective-permute-start | bytes 159752 | tf_op jit(solution)/shard_map/ppermute | solution.py:438
  6.7 4.1 %collective-permute-start = (bf16[1,104,256]{2,1,0:T(8,128)(2,1)S(1)}, bf16[1,104,256]{2,1,0:T(8,128)(2,1)S(1)}, u32[]{:S(2)}, u32[]{:S(2)}) collective-permute-start(bf16[1,104,256]{2,1,0:T(8,128)(2,1)S(1)} %pack.1), channel_id=1, source_target_pairs={{0,8},{4,12},{8,0},{12,4},{16,24},{20,28},{24,16},{28,20},{1,9},{5... | collective-permute-start | bytes 159752 | tf_op jit(solution)/shard_map/ppermute | solution.py:438
  11.8 11.9 %copy-start = (s32[4,12]{1,0:T(4,128)S(1)}, s32[4,12]{1,0:T(4,128)}, u32[]{:S(2)}) copy-start(s32[4,12]{1,0:T(4,128)} %live.1) | copy-start | bytes 580
  11.8 11.8 %copy-start.1 = (s32[4]{0:T(128)S(1)}, s32[4]{0:T(128)}, u32[]{:S(2)}) copy-start(s32[4]{0:T(128)} %lens.1) | copy-start | bytes 52
  11.8 5.1 %collective-permute-start.3 = (bf16[136,256]{1,0:T(8,128)(2,1)S(1)}, bf16[136,256]{1,0:T(8,128)(2,1)S(1)}, u32[]{:S(2)}, u32[]{:S(2)}) collective-permute-start(bf16[136,256]{1,0:T(8,128)(2,1)S(1)} %get-tuple-element.116), channel_id=1, source_target_pairs={{0,4},{4,0},{8,12},{12,8},{16,20},{20,16},{24,28},{28,24},{1,5},{5... | collective-permute-start | bytes 208904 | tf_op jit(solution)/shard_map/ppermute | solution.py:438
  13.4 7.2 %collective-permute-start.6 = (bf16[4,64,256]{2,1,0:T(8,128)(2,1)S(1)}, bf16[4,64,256]{2,1,0:T(8,128)(2,1)S(1)}, u32[]{:S(2)}, u32[]{:S(2)}) collective-permute-start(bf16[4,64,256]{2,1,0:T(8,128)(2,1)S(1)} %pad_maximum_fusion), channel_id=1, source_target_pairs={{0,4},{4,0},{8,12},{12,8},{16,20},{20,16},{24,28},{28,24},{1,5},{5... | collective-permute-start | bytes 393224 | tf_op jit(solution)/shard_map/ppermute | solution.py:438
  14.0 5.6 %collective-permute-start.4 = (bf16[4,64,256]{2,1,0:T(8,128)(2,1)S(1)}, bf16[4,64,256]{2,1,0:T(8,128)(2,1)S(1)}, u32[]{:S(2)}, u32[]{:S(2)}) collective-permute-start(bf16[4,64,256]{2,1,0:T(8,128)(2,1)S(1)} %pad_maximum_fusion), channel_id=1, source_target_pairs={{0,2},{1,3},{2,0},{3,1},{4,6},{5,7},{6,4},{7,5},{8,10},{9,11},{10,... | collective-permute-start | bytes 393224 | tf_op jit(solution)/shard_map/ppermute | solution.py:438
  16.9 5.1 %collective-permute-start.5 = (bf16[264,256]{1,0:T(8,128)(2,1)S(1)}, bf16[264,256]{1,0:T(8,128)(2,1)S(1)}, u32[]{:S(2)}, u32[]{:S(2)}) collective-permute-start(bf16[264,256]{1,0:T(8,128)(2,1)S(1)} %constant_dynamic-update-slice_fusion.5), channel_id=1, source_target_pairs={{0,2},{1,3},{2,0},{3,1},{4,6},{5,7},{6,4},{7,5},{8,10},{9,11},{10,... | collective-permute-start | bytes 405512 | tf_op jit(solution)/shard_map/ppermute | solution.py:438
  22.0 1.6 %collective-permute-start.7 = (bf16[520,256]{1,0:T(8,128)(2,1)S(1)}, bf16[520,256]{1,0:T(8,128)(2,1)S(1)}, u32[]{:S(2)}, u32[]{:S(2)}) collective-permute-start(bf16[520,256]{1,0:T(8,128)(2,1)S(1)} %constant_dynamic-update-slice_fusion.15.held), channel_id=1, source_target_pairs={{0,1},{1,0},{2,3},{3,2},{4,5},{5,4},{6,7},{7,6},{8,9},{9,8},{10,11... | collective-permute-start | bytes 798728 | tf_op jit(solution)/shard_map/ppermute | solution.py:438
  22.1 6.1 %collective-permute-start.10 = (bf16[8,64,256]{2,1,0:T(8,128)(2,1)S(1)}, bf16[8,64,256]{2,1,0:T(8,128)(2,1)S(1)}, u32[]{:S(2)}, u32[]{:S(2)}) collective-permute-start(bf16[8,64,256]{2,1,0:T(8,128)(2,1)S(1)} %constant_dynamic-update-slice_fusion.10.own), channel_id=1, source_target_pairs={{0,1},{1,0},{2,3},{3,2},{4,5},{5,4},{6,7},{7,6},{8,9},{9,8},{10,11... | collective-permute-start | bytes 786440 | tf_op jit(solution)/shard_map/ppermute | solution.py:438
  22.6 5.5 %collective-permute-start.8 = (bf16[4,64,256]{2,1,0:T(8,128)(2,1)S(1)}, bf16[4,64,256]{2,1,0:T(8,128)(2,1)S(1)}, u32[]{:S(2)}, u32[]{:S(2)}) collective-permute-start(bf16[4,64,256]{2,1,0:T(8,128)(2,1)S(1)} %collective-permute-done.4), channel_id=1, source_target_pairs={{0,4},{4,0},{8,12},{12,8},{16,20},{20,16},{24,28},{28,24},{1,5},{5... | collective-permute-start | bytes 393224 | tf_op jit(solution)/shard_map/ppermute | solution.py:438
  28.1 5.5 %collective-permute-start.9 = (bf16[8,64,256]{2,1,0:T(8,128)(2,1)S(1)}, bf16[8,64,256]{2,1,0:T(8,128)(2,1)S(1)}, u32[]{:S(2)}, u32[]{:S(2)}) collective-permute-start(bf16[8,64,256]{2,1,0:T(8,128)(2,1)S(1)} %constant_dynamic-update-slice_fusion.20.own), channel_id=1, source_target_pairs={{0,1},{1,0},{2,3},{3,2},{4,5},{5,4},{6,7},{7,6},{8,9},{9,8},{10,11... | collective-permute-start | bytes 786440 | tf_op jit(solution)/shard_map/ppermute | solution.py:438
  33.1 5.6 %collective-permute-start.12 = (bf16[8,64,256]{2,1,0:T(8,128)(2,1)S(1)}, bf16[8,64,256]{2,1,0:T(8,128)(2,1)S(1)}, u32[]{:S(2)}, u32[]{:S(2)}) collective-permute-start(bf16[8,64,256]{2,1,0:T(8,128)(2,1)S(1)} %get-tuple-element.90), channel_id=1, source_target_pairs={{0,1},{1,0},{2,3},{3,2},{4,5},{5,4},{6,7},{7,6},{8,9},{9,8},{10,11... | collective-permute-start | bytes 786440 | tf_op jit(solution)/shard_map/ppermute | solution.py:438
  38.7 8.1 %collective-permute-start.14 = (bf16[2304,256]{1,0:T(8,128)(2,1)S(1)}, bf16[2304,256]{1,0:T(8,128)(2,1)S(1)}, u32[]{:S(2)}, u32[]{:S(2)}) collective-permute-start(bf16[2304,256]{1,0:T(8,128)(2,1)S(1)} %get-tuple-element.97.y), channel_id=1, source_target_pairs={{0,1},{1,0},{2,3},{3,2},{4,5},{5,4},{6,7},{7,6},{8,9},{9,8},{10,11... | collective-permute-start | bytes 3538952 | tf_op jit(solution)/shard_map/ppermute | solution.py:438
  38.9 5.9 %collective-permute-start.13 = (bf16[4,64,256]{2,1,0:T(8,128)(2,1)S(1)}, bf16[4,64,256]{2,1,0:T(8,128)(2,1)S(1)}, u32[]{:S(2)}, u32[]{:S(2)}) collective-permute-start(bf16[4,64,256]{2,1,0:T(8,128)(2,1)S(1)} %slice.253), channel_id=1, source_target_pairs={{0,4},{4,0},{8,12},{12,8},{16,20},{20,16},{24,28},{28,24},{1,5},{5... | collective-permute-start | bytes 393224 | tf_op jit(solution)/shard_map/ppermute | solution.py:438
  43.9 1.8 %collective-permute-start.11 = (bf16[264,256]{1,0:T(8,128)(2,1)S(1)}, bf16[264,256]{1,0:T(8,128)(2,1)S(1)}, u32[]{:S(2)}, u32[]{:S(2)}) collective-permute-start(bf16[264,256]{1,0:T(8,128)(2,1)S(1)} %get-tuple-element.88), channel_id=1, source_target_pairs={{0,1},{1,0},{2,3},{3,2},{4,5},{5,4},{6,7},{7,6},{8,9},{9,8},{10,11... | collective-permute-start | bytes 405512 | tf_op jit(solution)/shard_map/ppermute | solution.py:438
  44.8 4.3 %collective-permute-start.16 = (bf16[2,64,256]{2,1,0:T(8,128)(2,1)S(1)}, bf16[2,64,256]{2,1,0:T(8,128)(2,1)S(1)}, u32[]{:S(2)}, u32[]{:S(2)}) collective-permute-start(bf16[2,64,256]{2,1,0:T(8,128)(2,1)S(1)} %slice.254), channel_id=1, source_target_pairs={{0,8},{4,12},{8,0},{12,4},{16,24},{20,28},{24,16},{28,20},{1,9},{5... | collective-permute-start | bytes 196616 | tf_op jit(solution)/shard_map/ppermute | solution.py:438
  45.8 4.4 %collective-permute-start.15 = (bf16[136,256]{1,0:T(8,128)(2,1)S(1)}, bf16[136,256]{1,0:T(8,128)(2,1)S(1)}, u32[]{:S(2)}, u32[]{:S(2)}) collective-permute-start(bf16[136,256]{1,0:T(8,128)(2,1)S(1)} %pad_maximum_fusion.1), channel_id=1, source_target_pairs={{0,4},{4,0},{8,12},{12,8},{16,20},{20,16},{24,28},{28,24},{1,5},{5... | collective-permute-start | bytes 208904 | tf_op jit(solution)/shard_map/ppermute | solution.py:438
  50.2 3.9 %collective-permute-start.17 = (bf16[2304,256]{1,0:T(8,128)(2,1)S(1)}, bf16[2304,256]{1,0:T(8,128)(2,1)S(1)}, u32[]{:S(2)}, u32[]{:S(2)}) collective-permute-start(bf16[2304,256]{1,0:T(8,128)(2,1)S(1)} %get-tuple-element.104), channel_id=1, source_target_pairs={{0,1},{1,0},{2,3},{3,2},{4,5},{5,4},{6,7},{7,6},{8,9},{9,8},{10,11... | collective-permute-start | bytes 3538952 | tf_op jit(solution)/shard_map/ppermute | solution.py:438
  50.4 7.7 %collective-permute-start.19 = (bf16[104,256]{1,0:T(8,128)(2,1)S(1)}, bf16[104,256]{1,0:T(8,128)(2,1)S(1)}, u32[]{:S(2)}, u32[]{:S(2)}) collective-permute-start(bf16[104,256]{1,0:T(8,128)(2,1)S(1)} %pad_maximum_fusion.2), channel_id=1, source_target_pairs={{0,16},{4,20},{8,24},{12,28},{16,0},{20,4},{24,8},{28,12},{1,17},{... | collective-permute-start | bytes 159752 | tf_op jit(solution)/shard_map/ppermute | solution.py:438
  52.3 5.6 %collective-permute-start.20 = (bf16[40,256]{1,0:T(8,128)(2,1)S(1)}, bf16[40,256]{1,0:T(8,128)(2,1)S(1)}, u32[]{:S(2)}, u32[]{:S(2)}) collective-permute-start(bf16[40,256]{1,0:T(8,128)(2,1)S(1)} %get-tuple-element.143), channel_id=1, source_target_pairs={{0,24},{4,28},{8,16},{12,20},{16,8},{20,12},{24,0},{28,4},{1,25},{... | collective-permute-start | bytes 61448 | tf_op jit(solution)/shard_map/ppermute | solution.py:438
  54.1 4.0 %collective-permute-start.18 = (bf16[40,256]{1,0:T(8,128)(2,1)S(1)}, bf16[40,256]{1,0:T(8,128)(2,1)S(1)}, u32[]{:S(2)}, u32[]{:S(2)}) collective-permute-start(bf16[40,256]{1,0:T(8,128)(2,1)S(1)} %get-tuple-element.144), channel_id=1, source_target_pairs={{0,8},{4,12},{8,0},{12,4},{16,24},{20,28},{24,16},{28,20},{1,9},{5... | collective-permute-start | bytes 61448 | tf_op jit(solution)/shard_map/ppermute | solution.py:438
